TPU v7x, 128 devices: a whole 4x4x4 slice. The times are simulated.
128 devices in a mesh: tx: 8 (over x_hi, z), ty: 16 (over x_lo, y, core).
Axes of the slice: x: 4 (x_hi: 2, x_lo: 2; x = x_hi * 2 + x_lo), y: 4, z: 4, core: 2. Of those that a mesh axis runs over, the one named last changes fastest.
Arguments:
- atm_state: bfloat16 [128, 512, 256], P('ty', 'tx'), may hold values from -6 to 6
- kernel_taps: float32 [3, 3, 256], replicated, may hold values from -2 to 2
- atm_gain: float32 [256], replicated, may hold values from 0.1 to 1.9
- atm_up: bfloat16 [256, 512], replicated, may hold values from -0.375 to 0.375
- atm_down: bfloat16 [512, 256], replicated, may hold values from -0.25 to 0.25
- couple_weight: bfloat16 [256, 128], replicated, may hold values from -0.375 to 0.375
- ocean_gain: float32 [128], replicated, may hold values from 0.1 to 1.9
- ocean_up: bfloat16 [128, 256], replicated, may hold values from -0.5 to 0.5
- ocean_down: bfloat16 [256, 128], replicated, may hold values from -0.375 to 0.375
- ocean_state: bfloat16 [32768, 32, 128], P(('tx', 'ty')), may hold values from -6 to 6
- land_mask: int32 [32768, 32], P(('tx', 'ty')), may hold values 0 or 1
- margin_cell: int32 [32768, 4, 32], P(('tx', 'ty')), may hold values from 0 to 511
- margin_area: float32 [32768, 4, 32], P(('tx', 'ty')), may hold values from 0.1 to 1
- owner_slot: int32 [32768], P(('tx', 'ty')), may hold values from 0 to 32767, as said below
- atm_cotangent: bfloat16 [128, 512, 256], P('ty', 'tx'), may hold values from -0.0234375 to 0.0234375
- ocean_cotangent: bfloat16 [32768, 32, 128], P(('tx', 'ty')), may hold values from -0.005859375 to 0.005859375
Outputs:
- atm_new: bfloat16 [128, 512, 256], P('ty', 'tx')
- ocean_new: bfloat16 [32768, 32, 128], P(('tx', 'ty'))
- grad_taps: float32 [3, 3, 256], replicated
- grad_atm_gain: float32 [256], replicated
- grad_atm_up: float32 [256, 512], replicated
- grad_atm_down: float32 [512, 256], replicated
- grad_couple: float32 [256, 128], replicated
- grad_ocean_gain: float32 [128], replicated
- grad_ocean_up: float32 [128, 256], replicated
- grad_ocean_down: float32 [256, 128], replicated
Inputs may be any that keep to these rules, and one draw needn't show every extreme that they name: Every slot number appears exactly once. Geographic block b lies under atmosphere tile b // 256; it is owned by device owner_slot[b] // 256 of tx+ty, device numbers being 16 * (tx index) + ty index. The blocks of one tile go to every device, exactly 2 to each.
All inputs are finite; a program needn't handle non-finite values. No bound on the sum of `land_mask` on one device may be relied on, other than what follows from the above.
Results may differ from a plain program's by a relative error of at most 0.008.
Values may be sent and summed in bfloat16 or wider, within the bound.
A program may use at most 128 MiB of HBM per device.

v0:
```python
import jax
import jax.numpy as jnp
from jax import lax
from jax.sharding import PartitionSpec as P

EPS = 1e-06


def padded(x, sides, width, wrap):
    for axis, dim in sides:
        peers, length = (lax.axis_size(axis), x.shape[dim])
        up = [(i, (i + 1) % peers) for i in range(peers if wrap else peers - 1)]
        down = [(j, i) for i, j in up]
        last = lax.slice_in_dim(x, length - width, length, axis=dim)
        leading = lax.slice_in_dim(x, 0, width, axis=dim)
        before = lax.ppermute(last, axis, up)
        after = lax.ppermute(leading, axis, down)
        x = jnp.concatenate([before, x, after], axis=dim)
    return x


def silu_grad(pre_act):
    logistic = jax.nn.sigmoid(pre_act)
    return logistic * (1.0 + pre_act * (1.0 - logistic))


def outer_sum(left, right):
    return lax.dot_general(
        left, right, (((0,), (0,)), ((), ())), preferred_element_type=jnp.float32
    )


def rms_norm(values, gain_vector):
    inverse_rms = lax.rsqrt(jnp.mean(values * values, axis=-1, keepdims=True) + EPS)
    unit_rows = values * inverse_rms
    return (unit_rows, inverse_rms, (unit_rows * gain_vector).astype(jnp.bfloat16))


def rms_back(normed_grad, unit_rows, inverse_rms, gain_vector):
    scaled = normed_grad * gain_vector
    gain_grad = jnp.sum(normed_grad * unit_rows, axis=0)
    inner_mean = jnp.mean(scaled * unit_rows, axis=-1, keepdims=True)
    return (inverse_rms * (scaled - unit_rows * inner_mean), gain_grad)


def stencil_sum(window, taps_array, height, breadth):
    running = jnp.zeros((height, breadth, window.shape[2]), jnp.float32)
    for lat_step in range(3):
        for lon_step in range(3):
            running = (
                running
                + taps_array[lat_step, lon_step]
                * window[lat_step : lat_step + height, lon_step : lon_step + breadth]
            )
    return running


def taps_grad(window, stencil_grad, height, breadth):
    rows_out = []
    for lat_step in range(3):
        for lon_step in range(3):
            rows_out.append(
                jnp.sum(
                    stencil_grad
                    * window[lat_step : lat_step + height, lon_step : lon_step + breadth],
                    axis=(0, 1),
                )
            )
    return jnp.stack(rows_out).reshape(3, 3, -1)


def mlp_forward(normed, up_weight, down_weight):
    pre_act = jnp.dot(normed, up_weight, preferred_element_type=jnp.float32)
    activation = jax.nn.silu(pre_act).astype(jnp.bfloat16)
    return (
        pre_act,
        activation,
        jnp.dot(activation, down_weight, preferred_element_type=jnp.float32),
    )


def mlp_backward(out_grad, normed, pre_act, activation, up_weight, down_weight):
    down_grad = outer_sum(activation, out_grad)
    act_grad = jnp.dot(out_grad, down_weight.T, preferred_element_type=jnp.float32)
    pre_grad = (act_grad * silu_grad(pre_act)).astype(jnp.bfloat16)
    up_grad = outer_sum(normed, pre_grad)
    normed_grad = jnp.dot(pre_grad, up_weight.T, preferred_element_type=jnp.float32)
    return (normed_grad, up_grad, down_grad)


def atm_forward(window, kernel_taps, atm_gain, atm_up, atm_down, height, breadth):
    channels = window.shape[2]
    stencil_rows = stencil_sum(window, kernel_taps, height, breadth).reshape(
        height * breadth, channels
    )
    unit_rows, inverse_rms, normed = rms_norm(stencil_rows, atm_gain)
    pre_act, activation, output = mlp_forward(normed, atm_up, atm_down)
    centre = window[1 : 1 + height, 1 : 1 + breadth].reshape(height * breadth, channels)
    fresh_rows = (centre.astype(jnp.float32) + output).astype(jnp.bfloat16)
    return (fresh_rows, (unit_rows, inverse_rms, normed, pre_act, activation))


def area_shares(margin_area):
    return margin_area / jnp.sum(margin_area, axis=1, keepdims=True)


def regrid(fresh_rows, margin_cell, shares):
    picked = fresh_rows[margin_cell]
    return jnp.sum(shares[..., None] * picked, axis=1).astype(jnp.bfloat16)


def regrid_back(mixed_grad, margin_cell, shares, count_cells):
    weighted = shares[..., None] * mixed_grad[:, None]
    return jax.ops.segment_sum(
        weighted.reshape(-1, weighted.shape[-1]), margin_cell.reshape(-1), num_segments=count_cells
    )


def project(mixed_rows, couple_weight):
    flat_rows = mixed_rows.reshape(-1, mixed_rows.shape[2])
    result = jnp.dot(flat_rows, couple_weight, preferred_element_type=jnp.float32).astype(
        jnp.bfloat16
    )
    return result.reshape(mixed_rows.shape[0], mixed_rows.shape[1], -1)


def project_back(flux_grad, couple_weight):
    flat_rows = flux_grad.reshape(-1, flux_grad.shape[2])
    result = jnp.dot(flat_rows, couple_weight.T, preferred_element_type=jnp.float32).astype(
        jnp.bfloat16
    )
    return result.reshape(flux_grad.shape[0], flux_grad.shape[1], -1)


def ocean_step(ocean_rows, flux_own, land_mask, cotangent, ocean_gain, ocean_up, ocean_down):
    channels = ocean_rows.shape[2]
    flat_state = ocean_rows.reshape(-1, channels)
    total_rows = flat_state.astype(jnp.float32) + flux_own.reshape(-1, channels).astype(jnp.float32)
    unit_rows, inverse_rms, normed = rms_norm(total_rows, ocean_gain)
    pre_act, activation, output = mlp_forward(normed, ocean_up, ocean_down)
    wet_cells = land_mask.reshape(-1, 1)
    fresh_rows = (flat_state.astype(jnp.float32) + wet_cells.astype(jnp.float32) * output).astype(
        jnp.bfloat16
    )
    out_grad = cotangent.reshape(-1, channels) * wet_cells.astype(cotangent.dtype)
    normed_grad, up_grad, down_grad = mlp_backward(
        out_grad, normed, pre_act, activation, ocean_up, ocean_down
    )
    total_grad, gain_grad = rms_back(normed_grad, unit_rows, inverse_rms, ocean_gain)
    return (
        fresh_rows.reshape(ocean_rows.shape),
        total_grad.astype(jnp.bfloat16).reshape(ocean_rows.shape),
        gain_grad,
        up_grad,
        down_grad,
    )


def bucket_rank(target, devices):
    onehot = (target[:, None] == jnp.arange(devices, dtype=jnp.int32)[None, :]).astype(jnp.int32)
    earlier = jnp.cumsum(onehot, axis=0) - onehot
    return jnp.sum(earlier * onehot, axis=1)


def body(
    atm_state,
    kernel_taps,
    atm_gain,
    atm_up,
    atm_down,
    couple_weight,
    ocean_gain,
    ocean_up,
    ocean_down,
    ocean_state,
    land_mask,
    margin_cell,
    margin_area,
    owner_slot,
    atm_cotangent,
    ocean_cotangent,
):
    height, breadth, channels = atm_state.shape
    blocks = ocean_state.shape[0]
    devices = lax.axis_size(("tx", "ty"))
    capacity = blocks // devices
    lat_wide = padded(atm_state, (("ty", 0),), 1, False)
    window = padded(lat_wide, (("tx", 1),), 1, True)
    fresh_rows, saved_parts = atm_forward(
        window, kernel_taps, atm_gain, atm_up, atm_down, height, breadth
    )
    unit_rows, inverse_rms, normed, pre_act, activation = saved_parts
    shares = area_shares(margin_area)
    mixed_rows = regrid(fresh_rows, margin_cell, shares)
    target = owner_slot // blocks
    send_slot = target * capacity + bucket_rank(target, devices)
    local_slot = owner_slot % blocks
    outgoing = project(mixed_rows, couple_weight)
    packed = (
        jnp.zeros((devices * capacity,) + outgoing.shape[1:], outgoing.dtype)
        .at[send_slot]
        .set(outgoing)
    )
    packed_slots = jnp.zeros((devices * capacity,), jnp.int32).at[send_slot].set(local_slot)
    arrived, arrived_slot = (
        lax.all_to_all(packed, ("tx", "ty"), split_axis=0, concat_axis=0, tiled=True),
        lax.all_to_all(packed_slots, ("tx", "ty"), split_axis=0, concat_axis=0, tiled=True),
    )
    placed = jnp.zeros_like(arrived).at[arrived_slot].set(arrived)
    ocean_new, flux_grad_own, ocean_gain_grad, ocean_up_grad, ocean_down_grad = ocean_step(
        ocean_state, placed, land_mask, ocean_cotangent, ocean_gain, ocean_up, ocean_down
    )
    packed_back = flux_grad_own[arrived_slot]
    returned = lax.all_to_all(packed_back, ("tx", "ty"), split_axis=0, concat_axis=0, tiled=True)[
        send_slot
    ]
    couple_grad = outer_sum(
        mixed_rows.reshape(-1, channels), returned.reshape(-1, returned.shape[2])
    )
    mixed_grad = project_back(returned, couple_weight)
    back_rows = regrid_back(mixed_grad, margin_cell, shares, height * breadth)
    out_grad = (atm_cotangent.reshape(-1, channels).astype(jnp.float32) + back_rows).astype(
        jnp.bfloat16
    )
    normed_grad, up_grad, down_grad = mlp_backward(
        out_grad, normed, pre_act, activation, atm_up, atm_down
    )
    stencil_grad, gain_grad = rms_back(normed_grad, unit_rows, inverse_rms, atm_gain)
    taps_part = taps_grad(window, stencil_grad.reshape(height, breadth, channels), height, breadth)
    summed = lax.psum(
        (
            taps_part,
            gain_grad,
            up_grad,
            down_grad,
            couple_grad,
            ocean_gain_grad,
            ocean_up_grad,
            ocean_down_grad,
        ),
        ("tx", "ty"),
    )
    return (
        fresh_rows.reshape(height, breadth, channels),
        ocean_new,
        summed[0],
        summed[1],
        summed[2],
        summed[3],
        summed[4],
        summed[5],
        summed[6],
        summed[7],
    )


def solution(mesh):
    return jax.shard_map(
        body,
        mesh=mesh,
        in_specs=(
            P("ty", "tx", None),
            P(),
            P(),
            P(),
            P(),
            P(),
            P(),
            P(),
            P(),
            P(("tx", "ty"), None, None),
            P(("tx", "ty"), None),
            P(("tx", "ty"), None, None),
            P(("tx", "ty"), None, None),
            P(("tx", "ty")),
            P("ty", "tx", None),
            P(("tx", "ty"), None, None),
        ),
        out_specs=(
            P("ty", "tx", None),
            P(("tx", "ty"), None, None),
            P(),
            P(),
            P(),
            P(),
            P(),
            P(),
            P(),
            P(),
        ),
        check_vma=False,
    )
```

profile of v0, /device:TPU:1, one launch (start us, length us, event | category | flops | bytes accessed | tf_op | source)
XLA Modules:
  0.0 697.3 jit_solution(15881913061801396319)
XLA Ops:
  7.2 0.7 and_select_fusion
  8.6 1.4 scatter_custom_fusion
  10.0 0.8 all_to_all.14
  10.8 11.5 %all-to-all-start = ((s32[128,2,1]{1,2,0:T(1,128)}), s32[128,2,1]{1,2,0:T(1,128)S(1)}, u32[]{:S(2)}, u32[]{:S(2)}) async-start(s32[128,2,1]{1,2,0:T(1,128)} %bitcast.17), calls=%async_computation | async-start | bytes 131072 | tf_op jit(solution)/shard_map/all_to_all | solution.py:207
  22.3 0.8 fusion.41
  23.0 3.0 collective-permute-start.1
  26.0 2.6 collective-permute-start
  28.6 0.9 reduce_sum.164
  29.5 0.9 broadcast_divide_fusion
  30.5 0.9 compare_select_fusion
  31.9 1.5 fusion.42
  33.4 1.0 constant_dynamic-update-slice_fusion.1
  34.4 1.6 collective-permute-start.2
  36.0 4.3 collective-permute-start.3
  40.8 0.5 collective-permute-done.2
  41.3 0.7 multiply_reduce_fusion.6
  42.1 0.6 copy-done.34
  43.2 1.6 fusion.6
  44.8 128.7 %gather_fusion = bf16[32768,256]{1,0:T(8,128)(2,1)} fusion(bf16[512,256]{1,0:T(8,128)(2,1)S(1)} %fusion.6, s32[32768]{0:T(1024)S(1)} %broadcast_clamp_fusion), kind=kCustom, calls=%fused_computation | custom fusion | bytes 33685504 | tf_op jit(solution)/shard_map/gather | solution.py:108
  173.4 11.5 %fusion = bf16[256,32,256]{2,1,0:T(8,128)(2,1)S(1)} fusion(bf16[256,4,32,256]{3,2,1,0:T(8,128)(2,1)} %bitcast.111, f32[256,4,32]{2,1,0:T(4,128)S(1)} %copy.41), kind=kLoop, calls=%fused_computation.8 | loop fusion | flops 23068672 | bytes 21102592 | tf_op jit(solution)/shard_map/reduce_sum | solution.py:109
  185.0 1.3 convolution_convert_fusion.1
  186.3 0.6 copy-done.6
  186.9 1.6 broadcast.112.clone
  188.5 26.5 %scatter_fusion = bf16[256,32,128]{2,1,0:T(8,128)(2,1)} fusion(bf16[256,32,128]{2,1,0:T(8,128)(2,1)} %broadcast.112.clone, s32[256]{0:T(256)S(1)} %compare_select_fusion.2, bf16[256,32,128]{2,1,0:T(8,128)(2,1)S(1)} %bitcast.116), kind=kCustom, calls=%fused_computation.4 | custom fusion | bytes 6292480 | tf_op jit(solution)/shard_map/scatter | solution.py:202
  215.0 11.3 %all-to-all-start.1 = ((bf16[256,32,128]{2,1,0:T(8,128)(2,1)}), bf16[256,32,128]{2,1,0:T(8,128)(2,1)}, u32[]{:S(2)}, u32[]{:S(2)}) async-start(bf16[256,32,128]{2,1,0:T(8,128)(2,1)} %scatter_fusion), calls=%async_computation.1 | async-start | bytes 4194304 | tf_op jit(solution)/shard_map/all_to_all | solution.py:206
  226.4 2.4 bitcast_multiply_fusion.1
  228.7 0.5 broadcast.166
  229.2 0.8 reduce.5
  230.2 26.2 %all-to-all-done.1 = bf16[256,32,128]{2,1,0:T(8,128)(2,1)} async-done(((bf16[256,32,128]{2,1,0:T(8,128)(2,1)}), bf16[256,32,128]{2,1,0:T(8,128)(2,1)}, u32[]{:S(2)}, u32[]{:S(2)}) %all-to-all-start.1) | async-done | bytes 2097184 | tf_op jit(solution)/shard_map/all_to_all | solution.py:206
  256.7 18.6 %scatter_fusion.1 = bf16[256,32,128]{2,1,0:T(8,128)(2,1)S(1)} fusion(bf16[256,32,128]{2,1,0:T(8,128)(2,1)S(1)} %broadcast.112, s32[256]{0:T(256)S(1)} %bitcast.125, bf16[256,32,128]{2,1,0:T(8,128)(2,1)} %all-to-all-done.1), kind=kCustom, calls=%fused_computation.5 | custom fusion | bytes 6292480 | tf_op jit(solution)/shard_map/scatter | solution.py:209
  275.3 2.8 multiply_reduce_fusion.2
  278.2 2.5 fusion.4
  280.8 3.9 multiply_convert_fusion
  284.7 3.4 fusion.1
  288.1 2.3 multiply_reduce_fusion
  290.4 5.5 multiply_convert_fusion.1
  296.0 3.8 gather_fusion.1
  299.7 5.6 all-to-all-start.2
  305.9 1.1 copy.43
  307.1 0.9 copy.37
  307.9 0.7 convert_element_type.170
  308.9 1.1 bitcast_convert_fusion
  310.0 4.3 fusion.46
  314.4 3.8 fusion.7
  318.2 17.4 %all-to-all-done.2 = bf16[256,32,128]{2,1,0:T(8,128)(2,1)} async-done(((bf16[256,32,128]{2,1,0:T(8,128)(2,1)}), bf16[256,32,128]{2,1,0:T(8,128)(2,1)}, u32[]{:S(2)}, u32[]{:S(2)}) %all-to-all-start.2) | async-done | bytes 2097184 | tf_op jit(solution)/shard_map/all_to_all | solution.py:214
  335.6 2.6 gather_fusion.2
  338.2 4.2 convolution_bitcast_fusion
  342.4 1.3 convolution_convert_fusion
  343.6 1.1 convert.7
  344.7 11.6 %bitcast_multiply_fusion = f32[32768,256]{1,0:T(8,128)} fusion(f32[256,32,256]{2,1,0:T(8,128)S(1)} %convert.7, f32[32768]{0:T(1024)S(1)} %mul.332), kind=kLoop, calls=%fused_computation.9 | loop fusion | flops 8388608 | bytes 42074112 | tf_op jit(solution)/shard_map/mul | solution.py:113
  356.3 175.7 %scatter_fusion.2 = f32[512,256]{1,0:T(8,128)S(1)} fusion(f32[512,256]{1,0:T(8,128)S(1)} %bitcast_convert_fusion, s32[32768]{0:T(1024)S(1)} %reshape.250, f32[32768,256]{1,0:T(8,128)} %bitcast_multiply_fusion), kind=kCustom, calls=%fused_computation.6 | custom fusion | flops 8388608 | bytes 100794368 | tf_op jit(solution)/shard_map/scatter-add | solution.py:114
  532.0 0.5 fusion.5
  532.6 0.7 copy-done.19
  533.3 1.3 fusion.32
  534.5 1.1 fusion.45
  535.8 4.1 fusion.3
  540.4 0.7 fusion.24
  541.2 63.4 %all-reduce = (f32[3,3,256]{2,1,0:T(4,128)}, f32[256]{0:T(256)}, f32[128]{0:T(128)}) all-reduce(f32[3,3,256]{2,1,0:T(4,128)S(1)} %reshape.194, f32[256]{0:T(256)S(1)} %get-tuple-element.12, f32[128]{0:T(128)S(1)} %copy-done.40), channel_id=1, replica_groups=mesh['tx'=8,'ty'=16] {'tx','ty'}, use_global_device_ids=true, to_apply=%region_22.23 | all-reduce | flops 2688 | bytes 21504 | tf_op jit(solution)/shard_map/psum | solution.py:230
  604.6 77.4 %all-reduce.4.cloned.1.call-done = (f32[256,512]{1,0:T(8,128)}, f32[512,256]{1,0:T(8,128)}, f32[256,128]{1,0:T(8,128)}, f32[128,256]{1,0:T(8,128)}, f32[256,128]{1,0:T(8,128)}) async-done(((f32[256,512]{1,0:T(8,128)}, f32[512,256]{1,0:T(8,128)}, f32[256,128]{1,0:T(8,128)}, f32[128,256]{1,0:T(8,128)}, f32[256,128]{1,0:T(8,128)}), (f32[256,512]{1,0:T(8,128)}, f32[512,256]{1,0:T(8,128)}, f32[256,128]{1,0:T(8,128)}, ...) | async-done | bytes 1441808 | tf_op jit(solution)/shard_map/psum | solution.py:230
  682.0 1.9 copy.56
  683.8 1.9 copy.57
  685.7 1.6 copy.58
  687.3 1.6 copy.59
  688.8 1.6 copy.60
  (125 shorter events, 4.1 us)
Async XLA Ops:
  7.2 35.7 %copy-start = (bf16[256,512]{1,0:T(8,128)(2,1)S(1)}, bf16[256,512]{1,0:T(8,128)(2,1)}, u32[]{:S(2)}) copy-start(bf16[256,512]{1,0:T(8,128)(2,1)} %param.19) | copy-start | bytes 786436
  7.2 34.1 %copy-start.10 = (bf16[8,64,256]{2,1,0:T(8,128)(2,1)S(1)}, bf16[8,64,256]{2,1,0:T(8,128)(2,1)}, u32[]{:S(2)}) copy-start(bf16[8,64,256]{2,1,0:T(8,128)(2,1)} %param.16) | copy-start | bytes 786436
  7.2 33.1 %copy-start.39 = (f32[3,3,256]{2,1,0:T(4,128)S(1)}, f32[3,3,256]{2,1,0:T(4,128)}, u32[]{:S(2)}) copy-start(f32[3,3,256]{2,1,0:T(4,128)} %param.17) | copy-start | bytes 27652
  7.2 35.5 %copy-start.36 = (f32[256]{0:T(256)S(1)}, f32[256]{0:T(256)}, u32[]{:S(2)}) copy-start(f32[256]{0:T(256)} %param.18) | copy-start | bytes 3076
  10.8 204.3 %all-to-all-start = ((s32[128,2,1]{1,2,0:T(1,128)}), s32[128,2,1]{1,2,0:T(1,128)S(1)}, u32[]{:S(2)}, u32[]{:S(2)}) async-start(s32[128,2,1]{1,2,0:T(1,128)} %bitcast.17), calls=%async_computation | async-start | bytes 131072 | tf_op jit(solution)/shard_map/all_to_all | solution.py:207
  23.0 11.3 %collective-permute-start.1 = (bf16[1,64,256]{2,1,0:T(8,128)(2,1)S(1)}, bf16[1,64,256]{2,1,0:T(8,128)(2,1)S(1)}, u32[]{:S(2)}, u32[]{:S(2)}) collective-permute-start(bf16[1,64,256]{2,1,0:T(8,128)(2,1)S(1)} %get-tuple-element.41), channel_id=1, source_target_pairs={{1,0},{2,1},{3,2},{4,3},{5,4},{6,5},{7,6},{8,7},{9,8},{10,9},{11,1... | collective-permute-start | bytes 98312 | tf_op jit(solution)/shard_map/ppermute | solution.py:17
  26.0 7.3 %collective-permute-start = (bf16[1,64,256]{2,1,0:T(8,128)(2,1)S(1)}, bf16[1,64,256]{2,1,0:T(8,128)(2,1)S(1)}, u32[]{:S(2)}, u32[]{:S(2)}) collective-permute-start(bf16[1,64,256]{2,1,0:T(8,128)(2,1)S(1)} %get-tuple-element.42), channel_id=1, source_target_pairs={{0,1},{1,2},{2,3},{3,4},{4,5},{5,6},{6,7},{7,8},{8,9},{9,10},{10,1... | collective-permute-start | bytes 98312 | tf_op jit(solution)/shard_map/ppermute | solution.py:16
  33.4 8.7 %copy-start.22 = (bf16[1,64,256]{2,1,0:T(8,128)(2,1)}, bf16[1,64,256]{2,1,0:T(8,128)(2,1)S(1)}, u32[]{:S(2)}) copy-start(bf16[1,64,256]{2,1,0:T(8,128)(2,1)S(1)} %collective-permute-done) | copy-start | bytes 98308
  34.4 7.7 %copy-start.20 = (bf16[1,64,256]{2,1,0:T(8,128)(2,1)}, bf16[1,64,256]{2,1,0:T(8,128)(2,1)S(1)}, u32[]{:S(2)}) copy-start(bf16[1,64,256]{2,1,0:T(8,128)(2,1)S(1)} %collective-permute-done.1) | copy-start | bytes 98308
  34.4 7.7 %copy-start.15 = (bf16[10,64,256]{2,1,0:T(8,128)(2,1)}, bf16[10,64,256]{2,1,0:T(8,128)(2,1)S(1)}, u32[]{:S(2)}) copy-start(bf16[10,64,256]{2,1,0:T(8,128)(2,1)S(1)} %constant_dynamic-update-slice_fusion) | copy-start | bytes 983044
  34.4 6.8 collective-permute-start.2
  36.0 5.3 collective-permute-start.3
  41.3 3.5 copy-start.30
  41.3 3.5 copy-start.32
  42.0 1.2 copy-start.8
  42.1 0.6 copy-start.34
  42.8 130.6 %copy-start.12 = (bf16[512,256]{1,0:T(8,128)(2,1)}, bf16[512,256]{1,0:T(8,128)(2,1)S(1)}, u32[]{:S(2)}) copy-start(bf16[512,256]{1,0:T(8,128)(2,1)S(1)} %multiply_convert_fusion.6) | copy-start | bytes 786436
  43.2 130.3 %copy-start.17 = (f32[512,512]{1,0:T(8,128)}, f32[512,512]{1,0:T(8,128)S(1)}, u32[]{:S(2)}) copy-start(f32[512,512]{1,0:T(8,128)S(1)} %fusion.44) | copy-start | bytes 3145732
  44.8 128.7 %copy-start.1 = (bf16[512,256]{1,0:T(8,128)(2,1)}, bf16[512,256]{1,0:T(8,128)(2,1)S(1)}, u32[]{:S(2)}) copy-start(bf16[512,256]{1,0:T(8,128)(2,1)S(1)} %fusion.6) | copy-start | bytes 786436
  173.4 11.6 %copy-start.24 = (bf16[256,128]{1,0:T(8,128)(2,1)S(1)}, bf16[256,128]{1,0:T(8,128)(2,1)}, u32[]{:S(2)}) copy-start(bf16[256,128]{1,0:T(8,128)(2,1)} %param.21) | copy-start | bytes 196612
  185.0 1.9 copy-start.6
  215.0 11.3 %copy-start.14 = (bf16[256,32,128]{2,1,0:T(8,128)(2,1)S(1)}, bf16[256,32,128]{2,1,0:T(8,128)(2,1)}, u32[]{:S(2)}) copy-start(bf16[256,32,128]{2,1,0:T(8,128)(2,1)} %param.31) | copy-start | bytes 6291460
  215.0 41.4 %all-to-all-start.1 = ((bf16[256,32,128]{2,1,0:T(8,128)(2,1)}), bf16[256,32,128]{2,1,0:T(8,128)(2,1)}, u32[]{:S(2)}, u32[]{:S(2)}) async-start(bf16[256,32,128]{2,1,0:T(8,128)(2,1)} %scatter_fusion), calls=%async_computation.1 | async-start | bytes 4194304 | tf_op jit(solution)/shard_map/all_to_all | solution.py:206
  278.2 2.5 copy-start.27
  278.2 2.5 copy-start.38
  280.8 9.7 %copy-start.2 = (f32[8192,128]{1,0:T(8,128)}, f32[8192,128]{1,0:T(8,128)S(1)}, u32[]{:S(2)}) copy-start(f32[8192,128]{1,0:T(8,128)S(1)} %fusion.4) | copy-start | bytes 12582916
  280.8 3.9 copy-start.7
  280.8 3.9 copy-start.28
  288.1 2.3 copy-start.4
  299.7 35.9 %all-to-all-start.2 = ((bf16[256,32,128]{2,1,0:T(8,128)(2,1)}), bf16[256,32,128]{2,1,0:T(8,128)(2,1)}, u32[]{:S(2)}, u32[]{:S(2)}) async-start(bf16[256,32,128]{2,1,0:T(8,128)(2,1)} %gather_fusion.1), calls=%async_computation.2 | async-start | bytes 4194304 | tf_op jit(solution)/shard_map/all_to_all | solution.py:214
  305.4 376.6 %all-reduce.4.cloned.1.call-start = ((), (), s32[]{:S(2)}) async-start(), calls=%async_computation.3 | async-start | bytes 2883584 | tf_op jit(solution)/shard_map/psum | solution.py:230
  308.9 5.5 copy-start.3
  338.2 4.2 copy-start.25
  356.3 175.7 %copy-start.18 = (f32[512,512]{1,0:T(8,128)S(1)}, f32[512,512]{1,0:T(8,128)}, u32[]{:S(2)}) copy-start(f32[512,512]{1,0:T(8,128)} %copy-done.17) | copy-start | bytes 3145732
  356.3 175.7 %copy-start.41 = (bf16[512,256]{1,0:T(8,128)(2,1)S(1)}, bf16[512,256]{1,0:T(8,128)(2,1)}, u32[]{:S(2)}) copy-start(bf16[512,256]{1,0:T(8,128)(2,1)} %param.20) | copy-start | bytes 786436
  532.0 1.2 copy-start.19
  532.0 2.5 copy-start.13
  533.2 2.4 copy-start.5
  533.2 2.4 copy-start.26
  533.3 2.5 copy-start.29
  535.7 4.2 copy-start.9
  535.7 4.2 copy-start.35
  535.7 4.2 copy-start.37
  535.7 4.6 copy-start.11
  535.8 4.6 copy-start.16
  535.8 4.6 copy-start.21
  535.8 4.6 copy-start.23
  535.8 4.6 copy-start.31
  535.8 4.6 copy-start.33
  535.8 5.4 copy-start.40
Sparse Core Ops, SparseCore 0:
  535.8 146.1 all-reduce.3
where the time goes:
time: 700 us; the launch traced here: 697 us
  other arithmetic  222 us (32%)
  local copies, waits for them, and re-layouts  202 us (29%)
  waiting for transfers between devices  122 us (17%)
  blocking collectives  63.4 us (9%)
  starting transfers between devices  40.1 us (6%)
  matrix products  33.7 us (5%)
  between operations  14.8 us (2%)
    scatter-add x1, other arithmetic, regrid_back(): jax.ops.segment_sum(weighted.reshape(-1, weighted.shape[-1]), margin_cell...  176 us
    gather x1, local copies, waits for them, and re-layouts, regrid(): picked = fresh_rows[margin_cell]  129 us
    psum x1, waiting for transfers between devices, body(): lax.psum((taps_part, gain_grad, up_grad, down_grad, couple_grad, ocean_ga...  77.4 us
    psum x1, blocking collectives, body(): lax.psum((taps_part, gain_grad, up_grad, down_grad, couple_grad, ocean_ga...  63.4 us
    scatter x1, local copies, waits for them, and re-layouts, body(): packed = jnp.zeros((devices * capacity,) + outgoing.shape[1:], outgoing.d...  26.5 us
    all_to_all x1, waiting for transfers between devices, body(): lax.all_to_all(packed, ('tx', 'ty'), split_axis=0, concat_axis=0, tiled=T...  26.2 us
    scatter x1, local copies, waits for them, and re-layouts, body(): placed = jnp.zeros_like(arrived).at[arrived_slot].set(arrived)  18.6 us
    all_to_all x1, waiting for transfers between devices, body(): lax.all_to_all(packed_back, ('tx', 'ty'), split_axis=0, concat_axis=0, ti...  17.4 us
  transfers between devices with their start and end apart: 8, of which 4 were waited for; matrix products, arithmetic and copies ran while one was open for 29% of the time, Pallas kernels for 0%

commit v1 on v0

v1 whole, which is shorter than its diff:
```python
import functools

import jax
import jax.numpy as jnp
from jax import lax
from jax.experimental import pallas as pl
from jax.experimental.pallas import tpu as pltpu
from jax.sharding import PartitionSpec as P

EPS = 1e-06
MESH = pl.DeviceIdType.MESH
F32, BF16, I32 = jnp.float32, jnp.bfloat16, jnp.int32
DEVICES = 128
MIX = 37
UNMIX = pow(MIX, -1, DEVICES)
ROWS = 64
GROUP = 8
GROUPS = DEVICES // GROUP


def digits(tx, ty):
    return (tx // 4) * 2 + ty // 8, (ty // 2) % 4, tx % 4, ty % 2


def offset_device(me, step, sign):
    code = (step * MIX) % DEVICES
    x = (me[0] + 4 + sign * ((code // 2) % 4)) % 4
    y = (me[1] + 4 + sign * ((code // 8) % 4)) % 4
    z = (me[2] + 4 + sign * (code // 32)) % 4
    c = (me[3] + code) % 2
    return ((x // 2) * 4 + z, (x % 2) * 8 + y * 2 + c)


def sigmoid(v):
    return 0.5 * jnp.tanh(0.5 * v) + 0.5


def dot(a, b):
    return jnp.dot(a, b, preferred_element_type=F32)


def dot_t(a, b):
    return lax.dot_general(a, b, (((1,), (1,)), ((), ())), preferred_element_type=F32)


def t_dot(a, b):
    return lax.dot_general(a, b, (((0,), (0,)), ((), ())), preferred_element_type=F32)


def loop(n, f):
    lax.fori_loop(0, n, lambda i, c: (f(i), c)[1], 0)


def kernel(
    atm, taps, again, up, down, couple, ogain, oup, odown, mask, cells, shares, slots_out, acot, ostate_hbm, ocot_hbm,
    anew, onew_hbm, gtaps, gagain, gup, gdown, gcouple, gogain, goup, godown,
    ostate, ocot, wet, spread, flux_out, flux_in, back_out, back_in, onew, onew_arr, slots_in, inv_v, slots_s, inv_s,
    win, unit, inv_rms, normed, pre, act, gather, sgrad,
    edge_w, edge_e, halo_n, halo_s, halo_c,
    load_sem, halo_ssem, halo_rsem, slot_ssem, slot_rsem, flux_ssem, flux_rsem, back_ssem, back_rsem, misc_sem,
):
    tx, ty = lax.axis_index("tx"), lax.axis_index("ty")
    me = digits(tx, ty)
    height, breadth = atm.shape[0], atm.shape[1]
    n_cells = height * breadth

    barrier = pltpu.get_barrier_semaphore()
    loads = [
        pltpu.make_async_copy(ostate_hbm, ostate, load_sem.at[0]),
        pltpu.make_async_copy(ocot_hbm, ocot, load_sem.at[1]),
    ]
    for load in loads:
        load.start()

    def greet(i):
        pl.semaphore_signal(barrier, inc=1, device_id=offset_device(me, i + 1, 1), device_id_type=MESH)

    loop(DEVICES - 1, greet)

    edge_w[...] = jnp.zeros_like(edge_w)
    edge_e[...] = jnp.zeros_like(edge_e)

    def own_rows(y):
        win[y + 1, 8 : 8 + breadth, :] = atm[y].astype(F32)

    loop(height, own_rows)
    west = jnp.concatenate([win[y + 1, 8:9, :] for y in range(height)], axis=0)
    east = jnp.concatenate([win[y + 1, 7 + breadth : 8 + breadth, :] for y in range(height)], axis=0)
    nothing = jnp.zeros_like(west)
    edge_w[...] = jnp.concatenate([west, nothing], axis=0).astype(BF16)
    edge_e[...] = jnp.concatenate([east, nothing], axis=0).astype(BF16)

    ones = jnp.ones((mask.shape[1], 128), BF16)

    def wet_rows(i):
        rows = lax.broadcasted_iota(I32, (512, 16), 0)
        cols = lax.broadcasted_iota(I32, (512, 16), 1)
        pick = (rows // 32 == cols).astype(F32).astype(BF16)
        wide = dot(pick, mask[pl.ds(pl.multiple_of(i * 16, 16), 16), :].astype(F32).astype(BF16))
        r2 = lax.broadcasted_iota(I32, wide.shape, 0)
        c2 = lax.broadcasted_iota(I32, wide.shape, 1)
        wide = jnp.where(r2 % 32 == c2, wide, 0.0).astype(BF16)
        wet[pl.ds(pl.multiple_of(i * 16, 16), 16)] = dot(wide, ones).astype(BF16).reshape(16, 32, 128)

    loop(16, wet_rows)

    def spread_columns(i):
        here = pl.ds(pl.multiple_of(i * 128, 128), 128)
        rows = lax.broadcasted_iota(I32, (n_cells, 128), 0)
        total = jnp.where(rows == cells[0:1, here], shares[0:1, here], 0.0)
        for k in range(1, 4):
            total = total + jnp.where(rows == cells[k : k + 1, here], shares[k : k + 1, here], 0.0)
        spread[:, here] = total.astype(BF16)

    loop(32, spread_columns)

    pl.semaphore_wait(barrier, DEVICES - 1)

    te, tw = (tx + 1) % 8, (tx + 7) % 8
    north, south = ty > 0, ty < 15

    def halo(i, src, dst, dx, dy):
        return pltpu.make_async_remote_copy(
            src, dst, halo_ssem.at[i], halo_rsem.at[i], device_id=(dx, dy), device_id_type=MESH
        )

    copies = [
        (south, halo(0, atm.at[height - 1], halo_n, tx, (ty + 1) % 16)),
        (north, halo(1, atm.at[0], halo_s, tx, (ty + 15) % 16)),
        (None, halo(2, edge_e, halo_c.at[0], te, ty)),
        (None, halo(3, edge_w, halo_c.at[1], tw, ty)),
        (south, halo(4, edge_e, halo_c.at[2], te, (ty + 1) % 16)),
        (south, halo(5, edge_w, halo_c.at[3], tw, (ty + 1) % 16)),
        (north, halo(6, edge_e, halo_c.at[4], te, (ty + 15) % 16)),
        (north, halo(7, edge_w, halo_c.at[5], tw, (ty + 15) % 16)),
    ]

    def when(cond, f):
        if cond is None:
            f()
        else:
            pl.when(cond)(f)

    for cond, copy in copies:
        when(cond, copy.start)

    def slot_copy(step, sign):
        return pltpu.make_async_remote_copy(
            slots_out.at[step], slots_in.at[step], slot_ssem, slot_rsem,
            device_id=offset_device(me, step, sign), device_id_type=MESH,
        )

    loop(DEVICES - 1, lambda i: slot_copy(i + 1, 1).start())
    slots_in[0] = slots_out[0]

    loop(32, lambda i: spread_columns(i + 32))

    for cond, copy in copies:
        when(cond, copy.wait_send)
    receives = [north, south, None, None, north, north, south, south]
    for cond, (_, copy) in zip(receives, copies):
        when(cond, copy.wait_recv)

    @pl.when(north)
    def _():
        win[0, 8 : 8 + breadth, :] = halo_n[...].astype(F32)
        win[0, 7:8, :] = halo_c[2].astype(F32)[height - 1 : height]
        win[0, 8 + breadth : 9 + breadth, :] = halo_c[3].astype(F32)[height - 1 : height]

    @pl.when(jnp.logical_not(north))
    def _():
        win[0] = jnp.zeros(win.shape[1:], F32)

    @pl.when(south)
    def _():
        win[height + 1, 8 : 8 + breadth, :] = halo_s[...].astype(F32)
        win[height + 1, 7:8, :] = halo_c[4].astype(F32)[0:1]
        win[height + 1, 8 + breadth : 9 + breadth, :] = halo_c[5].astype(F32)[0:1]

    @pl.when(jnp.logical_not(south))
    def _():
        win[height + 1] = jnp.zeros(win.shape[1:], F32)

    west, east = halo_c[0].astype(F32), halo_c[1].astype(F32)
    for y in range(height):
        win[y + 1, 7:8, :] = west[y : y + 1]
        win[y + 1, 8 + breadth : 9 + breadth, :] = east[y : y + 1]

    def stencil_row(y):
        total = jnp.zeros((breadth, 256), F32)
        for a in range(3):
            for b in range(3):
                total = total + taps[3 * a + b : 3 * a + b + 1, :] * win[y + a, 7 + b : 7 + b + breadth, :]
        inv = lax.rsqrt(jnp.mean(total * total, axis=-1, keepdims=True) + EPS)
        here = pl.ds(pl.multiple_of(y * breadth, breadth), breadth)
        u = total * inv
        unit[here, :] = u
        inv_rms[here, :] = jnp.broadcast_to(inv, (breadth, 128))
        normed[here, :] = (u * again[...]).astype(BF16)

    loop(height, stencil_row)

    def atm_mlp(i):
        here = pl.ds(pl.multiple_of(i * 128, 128), 128)
        v = dot(normed[here, :], up[...])
        pre[here, :] = v
        a = (v * sigmoid(v)).astype(BF16)
        act[here, :] = a
        old = atm[pl.ds(i * 2, 2)].reshape(128, 256).astype(F32)
        anew[pl.ds(i * 2, 2)] = (old + dot(a, down[...])).astype(BF16).reshape(2, breadth, 256)

    loop(4, atm_mlp)
    fresh = anew[...].reshape(n_cells, 256)
    coupled = dot(fresh, couple[...]).astype(BF16)
    gather[...] = coupled

    def flux_copy(step, sign):
        here = pl.ds(pl.multiple_of(step * ROWS, ROWS), ROWS)
        return pltpu.make_async_remote_copy(
            flux_out.at[here], flux_in.at[here], flux_ssem, flux_rsem.at[step // GROUP],
            device_id=offset_device(me, step, sign), device_id_type=MESH,
        )

    def flux_chunk(i):
        here = pl.ds(pl.multiple_of(i * 256, 256), 256)
        flux_out[here, :] = t_dot(spread[:, here], gather[...]).astype(BF16)
        for j in range(4):
            step = i * 4 + j
            if j == 0:
                pl.when(step > 0)(lambda: flux_copy(step, 1).start())
            else:
                flux_copy(step, 1).start()

    loop(DEVICES // 4, flux_chunk)
    flux_in[0:ROWS, :] = flux_out[0:ROWS, :]

    rest = slots_in.at[pl.ds(1, DEVICES - 1)]
    slots = pltpu.make_async_remote_copy(
        rest, rest, slot_ssem, slot_rsem, device_id=offset_device(me, 1, 1), device_id_type=MESH
    )
    slots.wait_recv()
    slots.wait_send()
    slot_rows = slots_in[...].reshape(DEVICES, 128)
    lane = lax.broadcasted_iota(I32, (DEVICES, 256), 1)
    step_row = lax.broadcasted_iota(I32, (DEVICES, 256), 0)
    found = jnp.where(slot_rows[:, 0:1] == lane, 2 * step_row, 0) + jnp.where(
        slot_rows[:, 1:2] == lane, 2 * step_row + 1, 0
    )
    inv_v[...] = jnp.broadcast_to(jnp.max(found, axis=0, keepdims=True), inv_v.shape)
    to_scalar = [
        pltpu.make_async_copy(slots_in, slots_s, misc_sem.at[0]),
        pltpu.make_async_copy(inv_v, inv_s, misc_sem.at[1]),
    ]
    for copy in to_scalar:
        copy.start()
    for copy in to_scalar:
        copy.wait()
    for load in loads:
        load.wait()

    goup[...] = jnp.zeros_like(goup)
    godown[...] = jnp.zeros_like(godown)
    gogain[...] = jnp.zeros_like(gogain)

    def back_copy(step, sign):
        here = pl.ds(pl.multiple_of(step * ROWS, ROWS), ROWS)
        return pltpu.make_async_remote_copy(
            back_out.at[here], back_in.at[here], back_ssem, back_rsem.at[step // GROUP],
            device_id=offset_device(me, step, sign), device_id_type=MESH,
        )

    def wait_group(g, buf, ssem, rsem):
        def first():
            some = buf.at[pl.ds(ROWS, (GROUP - 1) * ROWS)]
            pltpu.make_async_remote_copy(
                some, some, ssem, rsem.at[0], device_id=offset_device(me, 1, 1), device_id_type=MESH
            ).wait_recv()

        def later():
            some = buf.at[pl.ds(pl.multiple_of(g * (GROUP * ROWS), GROUP * ROWS), GROUP * ROWS)]
            pltpu.make_async_remote_copy(
                some, some, ssem, rsem.at[g], device_id=offset_device(me, 1, 1), device_id_type=MESH
            ).wait_recv()

        pl.when(g == 0)(first)
        pl.when(g > 0)(later)

    def ocean_group(g):
        wait_group(g, flux_in, flux_ssem, flux_rsem)
        here = pl.ds(pl.multiple_of(g * (GROUP * ROWS), GROUP * ROWS), GROUP * ROWS)
        slot = [slots_s[g * GROUP + j // 2, 0, j % 2] & 255 for j in range(2 * GROUP)]
        state = jnp.concatenate([ostate[s] for s in slot], axis=0).astype(F32)
        wets = jnp.concatenate([wet[s] for s in slot], axis=0)
        out_grad = jnp.concatenate([ocot[s] for s in slot], axis=0) * wets
        total = state + flux_in[here, :].astype(F32)
        inv = lax.rsqrt(jnp.mean(total * total, axis=-1, keepdims=True) + EPS)
        u = total * inv
        nrm = (u * ogain[...]).astype(BF16)
        v = dot(nrm, oup[...])
        s = sigmoid(v)
        a = (v * s).astype(BF16)
        onew_arr[pl.ds(g * (2 * GROUP), 2 * GROUP)] = (
            (state + wets.astype(F32) * dot(a, odown[...])).astype(BF16).reshape(2 * GROUP, 32, 128)
        )
        godown[...] += t_dot(a, out_grad)
        pg = (dot_t(out_grad, odown[...]) * (s * (1.0 + v * (1.0 - s)))).astype(BF16)
        goup[...] += t_dot(nrm, pg)
        ng = dot_t(pg, oup[...])
        gogain[...] += jnp.sum(ng * u, axis=0, keepdims=True)
        gg = ng * ogain[...]
        tg = inv * (gg - u * jnp.mean(gg * u, axis=-1, keepdims=True))
        back_out[here, :] = tg.astype(BF16)

        def send(j):
            step = g * GROUP + j
            pl.when(step > 0)(lambda: back_copy(step, -1).start())

        loop(GROUP, send)

    loop(GROUPS, ocean_group)
    back_in[0:ROWS, :] = back_out[0:ROWS, :]

    def place(i):
        for j in range(8):
            onew[i * 8 + j] = onew_arr[inv_s[0, i * 8 + j] & 255]

    loop(32, place)
    store = pltpu.make_async_copy(onew, onew_hbm, misc_sem.at[2])
    store.start()

    sgrad[:, 0:128] = jnp.zeros((n_cells, 128), F32)

    def back_group(g):
        wait_group(g, back_in, back_ssem, back_rsem)
        here = pl.ds(pl.multiple_of(g * (GROUP * ROWS), GROUP * ROWS), GROUP * ROWS)
        sgrad[:, 0:128] += dot(spread[:, here], back_in[here, :])

    loop(GROUPS, back_group)
    gathered = sgrad[:, 0:128].astype(BF16)
    gather[...] = gathered
    gcouple[...] = t_dot(anew[...].reshape(n_cells, 256), gathered)

    gup[...] = jnp.zeros_like(gup)
    gdown[...] = jnp.zeros_like(gdown)
    gagain[...] = jnp.zeros_like(gagain)
    gtaps[...] = jnp.zeros_like(gtaps)

    def atm_back(i):
        here = pl.ds(pl.multiple_of(i * 128, 128), 128)
        cot = acot[pl.ds(i * 2, 2)].reshape(128, 256).astype(F32)
        out_grad = (cot + dot_t(gather[here, :], couple[...])).astype(BF16)
        gdown[...] += t_dot(act[here, :], out_grad)
        v = pre[here, :]
        s = sigmoid(v)
        pg = (dot_t(out_grad, down[...]) * (s * (1.0 + v * (1.0 - s)))).astype(BF16)
        gup[...] += t_dot(normed[here, :], pg)
        ng = dot_t(pg, up[...])
        u = unit[here, :]
        gagain[...] += jnp.sum(ng * u, axis=0, keepdims=True)
        gg = ng * again[...]
        sgrad[here, :] = inv_rms[here, 0:1] * (gg - u * jnp.mean(gg * u, axis=-1, keepdims=True))

    loop(4, atm_back)

    def taps_row(y):
        sg = sgrad[pl.ds(pl.multiple_of(y * breadth, breadth), breadth), :]
        for a in range(3):
            for b in range(3):
                gtaps[3 * a + b : 3 * a + b + 1, :] += jnp.sum(
                    sg * win[y + a, 7 + b : 7 + b + breadth, :], axis=0, keepdims=True
                )

    loop(height, taps_row)

    sent = flux_out.at[pl.ds(ROWS, (DEVICES - 1) * ROWS)]
    pltpu.make_async_remote_copy(
        sent, sent, flux_ssem, flux_rsem.at[0], device_id=offset_device(me, 1, 1), device_id_type=MESH
    ).wait_send()
    sent = back_out.at[pl.ds(ROWS, (DEVICES - 1) * ROWS)]
    pltpu.make_async_remote_copy(
        sent, sent, back_ssem, back_rsem.at[0], device_id=offset_device(me, 1, 1), device_id_type=MESH
    ).wait_send()
    store.wait()


def body(
    atm_state, kernel_taps, atm_gain, atm_up, atm_down, couple_weight, ocean_gain, ocean_up, ocean_down,
    ocean_state, land_mask, margin_cell, margin_area, owner_slot, atm_cotangent, ocean_cotangent,
):
    height, breadth, channels = atm_state.shape
    blocks = ocean_state.shape[0]
    n_rows = blocks * 32

    target = owner_slot // blocks
    mine = digits(lax.axis_index("tx"), lax.axis_index("ty"))
    theirs = digits(target // 16, target % 16)
    dx, dy, dz, dc = [(t - m) % n for t, m, n in zip(theirs, mine, (4, 4, 4, 2))]
    step = ((((dz * 4 + dy) * 4 + dx) * 2 + dc) * UNMIX) % DEVICES
    index = jnp.arange(blocks, dtype=I32)
    earlier = (target[:, None] == target[None, :]) & (index[:, None] < index[None, :])
    place = 2 * step + jnp.sum(earlier.astype(I32), axis=0)
    order = (place[None, :] == index[:, None]).astype(F32)
    shares = margin_area / jnp.sum(margin_area, axis=1, keepdims=True)
    table = jnp.concatenate(
        [
            margin_cell.reshape(blocks, -1).astype(F32),
            shares.reshape(blocks, -1),
            (owner_slot % blocks).astype(F32)[:, None],
        ],
        axis=1,
    )
    table = jnp.dot(order, table, precision=lax.Precision.HIGHEST, preferred_element_type=F32)
    cells = jnp.round(table[:, :128]).astype(I32).reshape(blocks, 4, 32).transpose(1, 0, 2).reshape(4, n_rows)
    shares = table[:, 128:256].reshape(blocks, 4, 32).transpose(1, 0, 2).reshape(4, n_rows)
    slots = jnp.round(table[:, 256]).astype(I32).reshape(DEVICES, 1, 2)
    slots = jnp.pad(slots, ((0, 0), (0, 0), (0, 126)))

    vmem, any_ = pl.BlockSpec(memory_space=pltpu.VMEM), pl.BlockSpec(memory_space=pl.ANY)
    out_shape = [
        jax.ShapeDtypeStruct((height, breadth, channels), BF16),
        jax.ShapeDtypeStruct((blocks, 32, 128), BF16),
        jax.ShapeDtypeStruct((9, 256), F32),
        jax.ShapeDtypeStruct((1, 256), F32),
        jax.ShapeDtypeStruct((256, 512), F32),
        jax.ShapeDtypeStruct((512, 256), F32),
        jax.ShapeDtypeStruct((256, 128), F32),
        jax.ShapeDtypeStruct((1, 128), F32),
        jax.ShapeDtypeStruct((128, 256), F32),
        jax.ShapeDtypeStruct((256, 128), F32),
    ]
    block = lambda: pltpu.VMEM((blocks, 32, 128), BF16)
    flat = lambda: pltpu.VMEM((n_rows, 128), BF16)
    n_cells = height * breadth
    scratch = [
        block(), block(), block(),
        pltpu.VMEM((n_cells, n_rows), BF16),
        flat(), flat(), flat(), flat(),
        block(), block(),
        pltpu.VMEM((DEVICES, 1, 128), I32),
        pltpu.VMEM((8, 256), I32),
        pltpu.SMEM((DEVICES, 1, 128), I32),
        pltpu.SMEM((8, 256), I32),
        pltpu.VMEM((height + 2, breadth + 16, channels), F32),
        pltpu.VMEM((n_cells, 256), F32),
        pltpu.VMEM((n_cells, 128), F32),
        pltpu.VMEM((n_cells, 256), BF16),
        pltpu.VMEM((n_cells, 512), F32),
        pltpu.VMEM((n_cells, 512), BF16),
        pltpu.VMEM((n_cells, 128), BF16),
        pltpu.VMEM((n_cells, 256), F32),
        pltpu.VMEM((16, channels), BF16),
        pltpu.VMEM((16, channels), BF16),
        pltpu.VMEM((breadth, channels), BF16),
        pltpu.VMEM((breadth, channels), BF16),
        pltpu.VMEM((6, 16, channels), BF16),
        pltpu.SemaphoreType.DMA((2,)),
        pltpu.SemaphoreType.DMA((8,)),
        pltpu.SemaphoreType.DMA((8,)),
        pltpu.SemaphoreType.DMA,
        pltpu.SemaphoreType.DMA,
        pltpu.SemaphoreType.DMA,
        pltpu.SemaphoreType.DMA((GROUPS,)),
        pltpu.SemaphoreType.DMA,
        pltpu.SemaphoreType.DMA((GROUPS,)),
        pltpu.SemaphoreType.DMA((3,)),
    ]
    anew, onew, gtaps, *grads = pl.pallas_call(
        kernel,
        out_shape=out_shape,
        in_specs=[vmem] * 14 + [any_] * 2,
        out_specs=[vmem, any_] + [vmem] * 8,
        scratch_shapes=scratch,
        compiler_params=pltpu.CompilerParams(
            collective_id=0, has_side_effects=True, vmem_limit_bytes=56 * 1024 * 1024
        ),
    )(
        atm_state, kernel_taps.reshape(9, channels), atm_gain.reshape(1, -1), atm_up, atm_down, couple_weight,
        ocean_gain.reshape(1, -1), ocean_up, ocean_down, land_mask, cells, shares, slots,
        atm_cotangent, ocean_state, ocean_cotangent,
    )
    sums = lax.psum((gtaps, *grads), ("tx", "ty"))
    return (
        anew, onew, sums[0].reshape(3, 3, channels), sums[1].reshape(-1), sums[2], sums[3], sums[4],
        sums[5].reshape(-1), sums[6], sums[7],
    )


def solution(mesh):
    both = ("tx", "ty")
    return jax.shard_map(
        body,
        mesh=mesh,
        in_specs=(P("ty", "tx", None),) + (P(),) * 8 + (
            P(both, None, None), P(both, None), P(both, None, None), P(both, None, None), P(both),
            P("ty", "tx", None), P(both, None, None),
        ),
        out_specs=(P("ty", "tx", None), P(both, None, None)) + (P(),) * 8,
        check_vma=False,
    )
```

time: 700 us -> 275 us (0.39)
  other arithmetic: 222 us -> 3.66 us
  local copies, waits for them, and re-layouts: 202 us -> 15.2 us
  Pallas kernels: 0 us -> 92.6 us
  waiting for transfers between devices: 122 us -> 81.5 us
  starting transfers between devices: 40.1 us -> 0.04 us
  matrix products: 33.7 us -> 0.33 us
    scatter-add x1 -> x0, other arithmetic: 176 us -> none  [regrid_back(): jax.ops.segment_sum(weighted.reshape(-1, weighted.shape[-1]), margin_cell...]
    gather x3 -> x0, local copies, waits for them, and re-layouts: 135 us -> none  [the longest x1 129 us: regrid(): picked = fresh_rows[margin_cell]]
    pallas_call x0 -> x1, Pallas kernels: none -> 92.6 us  [body(): pl.pallas_call(kernel, out_shape=out_shape, in_specs=[vmem] * 14 + [any_]...]
    scatter x3 -> x0, local copies, waits for them, and re-layouts: 46.6 us -> none  [the longest x1 26.5 us: body(): packed = jnp.zeros((devices * capacity,) + outgoing.shape[1:], outgoing.d...]
    all_to_all x3 -> x0, waiting for transfers between devices: 43.6 us -> none  [the longest x1 26.2 us: body(): lax.all_to_all(packed, ('tx', 'ty'), split_axis=0, concat_axis=0, tiled=T...]
    dot_general x15 -> x1, matrix products: 33.7 us -> 0.33 us  [body(): jnp.dot(order, table, precision=lax.Precision.HIGHEST, preferred_element_...]
    all_to_all x3 -> x0, starting transfers between devices: 28.4 us -> none  [the longest x1 11.5 us: body(): lax.all_to_all(packed_slots, ('tx', 'ty'), split_axis=0, concat_axis=0, t...]
    mul x3 -> x0, other arithmetic: 16.5 us -> none  [the longest x1 11.6 us: regrid_back(): weighted = shares[..., None] * mixed_grad[:, None]]
  transfers between devices with their start and end apart: 8 -> 1, of which waited for: 4 -> 1; matrix products, arithmetic and copies ran while one was open for 29% -> 0% of each run, Pallas kernels for 0% -> 0%
where the time goes in v1:
time: 275 us
  Pallas kernels  92.6 us (34%)
  waiting for transfers between devices  81.5 us (30%)
  blocking collectives  67 us (24%)
  local copies, waits for them, and re-layouts  15.2 us (6%)
  between operations  14.2 us (5%)
  other arithmetic  3.66 us (1%)
    pallas_call x1, Pallas kernels, body(): pl.pallas_call(kernel, out_shape=out_shape, in_specs=[vmem] * 14 + [any_]...  92.6 us
    psum x1, waiting for transfers between devices, body(): sums = lax.psum((gtaps, *grads), ('tx', 'ty'))  81.5 us
    psum x1, blocking collectives, body(): sums = lax.psum((gtaps, *grads), ('tx', 'ty'))  67 us
    unnamed x18, local copies, waits for them, and re-layouts  10.1 us
  transfers between devices with their start and end apart: 1, of which 1 were waited for; matrix products, arithmetic and copies ran while one was open for 0% of the time, Pallas kernels for 0%

profile of v1, /device:TPU:1, one launch (start us, length us, event | category | flops | bytes accessed | tf_op | source)
XLA Modules:
  0.0 274.6 jit_solution(4406379806793526379)
XLA Ops:
  7.2 0.0 all-reduce.5.cloned.1.call-start
  7.3 0.7 and_select_fusion.14
  8.0 0.1 convert_reduce_fusion
  8.1 0.9 reduce_sum.19
  9.0 0.9 broadcast_divide_fusion
  9.9 0.9 convert_element_type.30
  10.9 0.1 fusion.17
  10.9 0.3 fusion
  11.3 1.3 reshape.75.taps
  12.6 1.5 copy.36.mask
  14.2 0.1 convert_element_type.35
  14.3 0.7 pad.4.slots_out
  15.0 0.2 copy.33
  15.2 0.9 reshape.80.cells
  16.1 0.2 copy.34
  16.3 0.9 reshape.82.shares
  17.2 92.6 %shard_map.231 = (bf16[8,64,256]{2,1,0:T(8,128)(2,1)}, bf16[256,32,128]{2,1,0:T(8,128)(2,1)}, f32[9,256]{1,0:T(8,128)}, f32[1,256]{1,0:T(1,128)}, f32[256,512]{1...) custom-call(bf16[8,64,256]{2,1,0:T(8,128)(2,1)} %atm.1, ...), custom_call_target="tpu_custom_call" | custom-call | tf_op jit(solution)/shard_map/pallas_call | solution.py:467
  109.8 0.0 all-reduce.5.cloned.1.call-update
  109.8 0.7 reshape.83
  110.6 67.0 %all-reduce.1 = (f32[3,3,256]{2,1,0:T(4,128)}, f32[256]{0:T(256)}, f32[128]{0:T(128)}) all-reduce(f32[3,3,256]{2,1,0:T(4,128)S(1)} %reshape.83, f32[256]{0:T(256)} %bitcast.21, f32[128]{0:T(128)} %bitcast.23), channel_id=1, replica_groups=mesh['tx'=8,'ty'=16] {'tx','ty'}, use_global_device_ids=true, to_apply=%region_2.3 | all-reduce | flops 2688 | bytes 21504 | tf_op jit(solution)/shard_map/psum | solution.py:481
  177.6 81.5 %all-reduce.5.cloned.1.call-done = (f32[256,512]{1,0:T(8,128)}, f32[512,256]{1,0:T(8,128)}, f32[256,128]{1,0:T(8,128)}, f32[128,256]{1,0:T(8,128)}, f32[256,128]{1,0:T(8,128)}) async-done(((f32[256,512]{1,0:T(8,128)}, f32[512,256]{1,0:T(8,128)}, f32[256,128]{1,0:T(8,128)}, f32[128,256]{1,0:T(8,128)}, f32[256,128]{1,0:T(8,128)}), (f32[256,512]{1,0:T(8,128)}, f32[512,256]{1,0:T(8,128)}, f32[256,128]{1,0:T(8,128)}, ...) | async-done | bytes 1441808 | tf_op jit(solution)/shard_map/psum | solution.py:481
  259.1 1.7 copy.49
  260.8 0.0 copy-start.1
  260.8 0.0 copy-start
  260.8 3.4 %copy.50 = bf16[256,32,128]{2,1,0:T(8,128)(2,1)} copy(bf16[256,32,128]{2,1,0:T(8,128)(2,1)} %get-tuple-element.53) | data formatting | bytes 4194304
  264.1 0.0 copy-done.1
  264.1 0.0 copy-start.4
  264.1 0.0 copy-start.3
  264.2 0.0 copy-start.2
  264.2 0.8 copy.51
  265.0 0.0 copy-done
  265.0 0.8 copy.52
  265.8 0.0 copy-done.4
  265.8 0.7 copy.53
  266.4 0.0 copy-done.3
  266.4 0.7 copy.54
  267.1 0.0 copy-done.2
  267.1 0.7 copy.55
  (2 shorter events, 0.0 us)
Async XLA Ops:
  7.2 251.9 %all-reduce.5.cloned.1.call-start = ((), (), s32[]{:S(2)}) async-start(), calls=%async_computation | async-start | bytes 2883584 | tf_op jit(solution)/shard_map/psum | solution.py:481
  260.8 3.4 %copy-start.1 = (f32[256,512]{1,0:T(8,128)S(1)}, f32[256,512]{1,0:T(8,128)}, u32[]{:S(2)}) copy-start(f32[256,512]{1,0:T(8,128)} %get-tuple-element.56) | copy-start | bytes 1572868
  260.8 4.2 %copy-start = (f32[512,256]{1,0:T(8,128)S(1)}, f32[512,256]{1,0:T(8,128)}, u32[]{:S(2)}) copy-start(f32[512,256]{1,0:T(8,128)} %get-tuple-element.57) | copy-start | bytes 1572868
  264.1 1.6 copy-start.4
  264.1 2.3 copy-start.3
  264.2 2.9 %copy-start.2 = (f32[256,128]{1,0:T(8,128)S(1)}, f32[256,128]{1,0:T(8,128)}, u32[]{:S(2)}) copy-start(f32[256,128]{1,0:T(8,128)} %get-tuple-element.61) | copy-start | bytes 393220
Sparse Core Ops, SparseCore 0:
  110.0 149.1 all-reduce.4

commit v2 on v1

--- a/solution.py
+++ b/solution.py
@@ -16,6 +16,10 @@
 ROWS = 64
 GROUP = 8
 GROUPS = DEVICES // GROUP
+PIECE = 32
+OWNERS = 89
+AT_OUP, AT_ODOWN, AT_COUPLE, AT_SMALL, AT_DOWN, AT_UP = 0, 256, 512, 768, 800, 1824
+PACKED = OWNERS * PIECE
 
 
 def digits(tx, ty):
@@ -31,6 +35,10 @@
     return ((x // 2) * 4 + z, (x % 2) * 8 + y * 2 + c)
 
 
+def owner_rank(tx, ty):
+    return ((tx * 16 + ty) * MIX) % DEVICES
+
+
 def sigmoid(v):
     return 0.5 * jnp.tanh(0.5 * v) + 0.5
 
@@ -52,12 +60,14 @@
 
 
 def kernel(
-    atm, taps, again, up, down, couple, ogain, oup, odown, mask, cells, shares, slots_out, acot, ostate_hbm, ocot_hbm,
-    anew, onew_hbm, gtaps, gagain, gup, gdown, gcouple, gogain, goup, godown,
-    ostate, ocot, wet, spread, flux_out, flux_in, back_out, back_in, onew, onew_arr, slots_in, inv_v, slots_s, inv_s,
+    atm, taps, again, up, down, couple, ogain, oup, odown, mask, margin_cell, margin_area, owner, acot, ostate_hbm, ocot_hbm,
+    anew, onew_hbm, inv_v, packed_hbm,
+    ostate, ocot, wet, cells, shares, spread, flux_out, flux_in, back_out, back_in, onew_arr, slots_out, slots_in, slots_s,
     win, unit, inv_rms, normed, pre, act, gather, sgrad,
+    gtaps, gagain, gup, gdown, gogain, goup, godown, small, partial, pieces, packed,
     edge_w, edge_e, halo_n, halo_s, halo_c,
     load_sem, halo_ssem, halo_rsem, slot_ssem, slot_rsem, flux_ssem, flux_rsem, back_ssem, back_rsem, misc_sem,
+    part_ssem, part_rsem, sum_ssem, sum_rsem,
 ):
     tx, ty = lax.axis_index("tx"), lax.axis_index("ty")
     me = digits(tx, ty)
@@ -90,29 +100,69 @@
     edge_w[...] = jnp.concatenate([west, nothing], axis=0).astype(BF16)
     edge_e[...] = jnp.concatenate([east, nothing], axis=0).astype(BF16)
 
-    ones = jnp.ones((mask.shape[1], 128), BF16)
+    slot = owner[...]
+    t_tx, t_ty = slot >> 12, (slot >> 8) & 15
+    theirs = ((t_tx >> 2) * 2 + (t_ty >> 3), (t_ty >> 1) & 3, t_tx & 3, t_ty & 1)
+    dx, dy, dz, dc = [(t - m + n) & (n - 1) for t, m, n in zip(theirs, me, (4, 4, 4, 2))]
+    step = ((((dz * 4 + dy) * 4 + dx) * 2 + dc) * UNMIX) & (DEVICES - 1)
+    blocks = slot.shape[1]
+    square = jnp.broadcast_to(step, (blocks, blocks))
+    first = lax.broadcasted_iota(I32, square.shape, 0)
+    second = lax.broadcasted_iota(I32, square.shape, 1)
+    same = (square.astype(F32).T == square.astype(F32)) & (first < second)
+    place = 2 * step + jnp.sum(same.astype(F32), axis=0, keepdims=True).astype(I32)
+
+    steps = lax.broadcasted_iota(I32, (DEVICES, blocks), 0)
+    local = jnp.broadcast_to(slot & (blocks - 1), (DEVICES, blocks))
+    lanes = lax.broadcasted_iota(I32, (DEVICES, 128), 1)
+    pair = [
+        jnp.sum(jnp.where(place == 2 * steps + j, local, 0).astype(F32), axis=1, keepdims=True).astype(I32)
+        for j in range(2)
+    ]
+    slots_out[...] = jnp.where(lanes == 0, pair[0], pair[1])
+
+    area = margin_area[...]
+    share = (area / jnp.sum(area, axis=0, keepdims=True)).reshape(128, blocks).astype(BF16)
+    cell = margin_cell[...].reshape(128, blocks)
+    high, low = (cell >> 4).astype(F32).astype(BF16), (cell & 15).astype(F32).astype(BF16)
+    quads = lax.broadcasted_iota(I32, (blocks // 4, blocks), 0)
+    lane_block = lax.broadcasted_iota(I32, (blocks // 4, 128), 1) // 32
+    got_share = [jnp.zeros((blocks // 4, 128), F32)] * 4
+    got_cell = [jnp.zeros((blocks // 4, 128), F32)] * 4
+    for j in range(4):
+        pick = (place == 4 * quads + j).astype(F32).astype(BF16)
+        one_share = dot_t(pick, share)
+        one_cell = 16.0 * dot_t(pick, high) + dot_t(pick, low)
+        for k in range(4):
+            turn = (32 * (j - k)) % 128
+            here = lane_block == j
+            got_share[k] = jnp.where(here, pltpu.roll(one_share, turn, 1) if turn else one_share, got_share[k])
+            got_cell[k] = jnp.where(here, pltpu.roll(one_cell, turn, 1) if turn else one_cell, got_cell[k])
+    for k in range(4):
+        shares[k] = got_share[k]
+        cells[k] = got_cell[k].astype(I32)
+
+    ones = jnp.ones((32, 128), BF16)
+    wet_rows_of = mask[...].astype(F32).astype(BF16)
 
     def wet_rows(i):
-        rows = lax.broadcasted_iota(I32, (512, 16), 0)
-        cols = lax.broadcasted_iota(I32, (512, 16), 1)
-        pick = (rows // 32 == cols).astype(F32).astype(BF16)
-        wide = dot(pick, mask[pl.ds(pl.multiple_of(i * 16, 16), 16), :].astype(F32).astype(BF16))
+        rows = lax.broadcasted_iota(I32, (512, blocks), 0)
+        cols = lax.broadcasted_iota(I32, (512, blocks), 1)
+        pick = (rows // 32 + i * 16 == cols).astype(F32).astype(BF16)
+        wide = dot_t(pick, wet_rows_of)
         r2 = lax.broadcasted_iota(I32, wide.shape, 0)
         c2 = lax.broadcasted_iota(I32, wide.shape, 1)
         wide = jnp.where(r2 % 32 == c2, wide, 0.0).astype(BF16)
         wet[pl.ds(pl.multiple_of(i * 16, 16), 16)] = dot(wide, ones).astype(BF16).reshape(16, 32, 128)
 
-    loop(16, wet_rows)
-
     def spread_columns(i):
         here = pl.ds(pl.multiple_of(i * 128, 128), 128)
         rows = lax.broadcasted_iota(I32, (n_cells, 128), 0)
-        total = jnp.where(rows == cells[0:1, here], shares[0:1, here], 0.0)
+        row = pl.ds(i, 1)
+        total = jnp.where(rows == cells[0, row, :], shares[0, row, :], 0.0)
         for k in range(1, 4):
-            total = total + jnp.where(rows == cells[k : k + 1, here], shares[k : k + 1, here], 0.0)
+            total = total + jnp.where(rows == cells[k, row, :], shares[k, row, :], 0.0)
         spread[:, here] = total.astype(BF16)
-
-    loop(32, spread_columns)
 
     pl.semaphore_wait(barrier, DEVICES - 1)
 
@@ -146,14 +196,15 @@
 
     def slot_copy(step, sign):
         return pltpu.make_async_remote_copy(
-            slots_out.at[step], slots_in.at[step], slot_ssem, slot_rsem,
+            slots_out.at[pl.ds(step, 1)], slots_in.at[pl.ds(step, 1)], slot_ssem, slot_rsem,
             device_id=offset_device(me, step, sign), device_id_type=MESH,
         )
 
     loop(DEVICES - 1, lambda i: slot_copy(i + 1, 1).start())
-    slots_in[0] = slots_out[0]
-
-    loop(32, lambda i: spread_columns(i + 32))
+    slots_in[0:1, :] = slots_out[0:1, :]
+
+    loop(64, spread_columns)
+    loop(16, wet_rows)
 
     for cond, copy in copies:
         when(cond, copy.wait_send)
@@ -190,7 +241,7 @@
         total = jnp.zeros((breadth, 256), F32)
         for a in range(3):
             for b in range(3):
-                total = total + taps[3 * a + b : 3 * a + b + 1, :] * win[y + a, 7 + b : 7 + b + breadth, :]
+                total = total + taps[a, b : b + 1, :] * win[y + a, 7 + b : 7 + b + breadth, :]
         inv = lax.rsqrt(jnp.mean(total * total, axis=-1, keepdims=True) + EPS)
         here = pl.ds(pl.multiple_of(y * breadth, breadth), breadth)
         u = total * inv
@@ -240,21 +291,16 @@
     )
     slots.wait_recv()
     slots.wait_send()
-    slot_rows = slots_in[...].reshape(DEVICES, 128)
+    slot_rows = slots_in[...]
     lane = lax.broadcasted_iota(I32, (DEVICES, 256), 1)
     step_row = lax.broadcasted_iota(I32, (DEVICES, 256), 0)
     found = jnp.where(slot_rows[:, 0:1] == lane, 2 * step_row, 0) + jnp.where(
         slot_rows[:, 1:2] == lane, 2 * step_row + 1, 0
     )
     inv_v[...] = jnp.broadcast_to(jnp.max(found, axis=0, keepdims=True), inv_v.shape)
-    to_scalar = [
-        pltpu.make_async_copy(slots_in, slots_s, misc_sem.at[0]),
-        pltpu.make_async_copy(inv_v, inv_s, misc_sem.at[1]),
-    ]
-    for copy in to_scalar:
-        copy.start()
-    for copy in to_scalar:
-        copy.wait()
+    to_scalar = pltpu.make_async_copy(slots_in, slots_s, misc_sem.at[0])
+    to_scalar.start()
+    to_scalar.wait()
     for load in loads:
         load.wait()
 
@@ -288,7 +334,7 @@
     def ocean_group(g):
         wait_group(g, flux_in, flux_ssem, flux_rsem)
         here = pl.ds(pl.multiple_of(g * (GROUP * ROWS), GROUP * ROWS), GROUP * ROWS)
-        slot = [slots_s[g * GROUP + j // 2, 0, j % 2] & 255 for j in range(2 * GROUP)]
+        slot = [slots_s[g * GROUP + j // 2, j % 2] & 255 for j in range(2 * GROUP)]
         state = jnp.concatenate([ostate[s] for s in slot], axis=0).astype(F32)
         wets = jnp.concatenate([wet[s] for s in slot], axis=0)
         out_grad = jnp.concatenate([ocot[s] for s in slot], axis=0) * wets
@@ -320,13 +366,11 @@
     loop(GROUPS, ocean_group)
     back_in[0:ROWS, :] = back_out[0:ROWS, :]
 
-    def place(i):
-        for j in range(8):
-            onew[i * 8 + j] = onew_arr[inv_s[0, i * 8 + j] & 255]
-
-    loop(32, place)
-    store = pltpu.make_async_copy(onew, onew_hbm, misc_sem.at[2])
+    store = pltpu.make_async_copy(onew_arr, onew_hbm, misc_sem.at[1])
     store.start()
+    partial[AT_OUP : AT_OUP + 128, :] = goup[:, 0:128].astype(BF16)
+    partial[AT_OUP + 128 : AT_OUP + 256, :] = goup[:, 128:256].astype(BF16)
+    partial[AT_ODOWN : AT_ODOWN + 256, :] = godown[...].astype(BF16)
 
     sgrad[:, 0:128] = jnp.zeros((n_cells, 128), F32)
 
@@ -338,7 +382,7 @@
     loop(GROUPS, back_group)
     gathered = sgrad[:, 0:128].astype(BF16)
     gather[...] = gathered
-    gcouple[...] = t_dot(anew[...].reshape(n_cells, 256), gathered)
+    partial[AT_COUPLE : AT_COUPLE + 256, :] = t_dot(anew[...].reshape(n_cells, 256), gathered).astype(BF16)
 
     gup[...] = jnp.zeros_like(gup)
     gdown[...] = jnp.zeros_like(gdown)
@@ -372,6 +416,71 @@
 
     loop(height, taps_row)
 
+    small[...] = jnp.zeros_like(small)
+    small[0:9, :] = gtaps[0:9, 0:128]
+    small[9:18, :] = gtaps[0:9, 128:256]
+    small[18:19, :] = gagain[:, 0:128]
+    small[19:20, :] = gagain[:, 128:256]
+    small[20:21, :] = gogain[...]
+    partial[AT_SMALL : AT_SMALL + 32, :] = small[...].astype(BF16)
+    for i in range(2):
+        partial[AT_DOWN + 512 * i : AT_DOWN + 512 * (i + 1), :] = gdown[:, 128 * i : 128 * (i + 1)].astype(BF16)
+    for i in range(4):
+        partial[AT_UP + 256 * i : AT_UP + 256 * (i + 1), :] = gup[:, 128 * i : 128 * (i + 1)].astype(BF16)
+
+    def rows_of(rank):
+        return pl.ds(pl.multiple_of(rank * PIECE, PIECE), PIECE)
+
+    def part_copy(step):
+        to = offset_device(me, step, 1)
+        rank = owner_rank(*to)
+        return rank, pltpu.make_async_remote_copy(
+            partial.at[rows_of(rank)], pieces.at[step], part_ssem, part_rsem, device_id=to, device_id_type=MESH
+        )
+
+    def send_part(i):
+        rank = owner_rank(*offset_device(me, i + 1, 1))
+        pl.when(rank < OWNERS)(lambda: part_copy(i + 1)[1].start())
+
+    loop(DEVICES - 1, send_part)
+    rank = owner_rank(tx, ty)
+    owns = rank < OWNERS
+
+    def both_ends(ref, ssem, rsem):
+        return pltpu.make_async_remote_copy(
+            ref, ref, ssem, rsem, device_id=offset_device(me, 1, 1), device_id_type=MESH
+        )
+
+    @pl.when(owns)
+    def _():
+        both_ends(pieces.at[pl.ds(1, DEVICES - 1)], part_ssem, part_rsem).wait_recv()
+        pieces[0] = partial[rows_of(rank), :]
+
+        def add(i, total):
+            return total + jnp.sum(pieces[pl.ds(i * 8, 8)].astype(F32), axis=0)
+
+        total = lax.fori_loop(0, DEVICES // 8, add, jnp.zeros((PIECE, 128), F32))
+        packed[rows_of(rank), :] = total.astype(BF16)
+
+        def send_sum(i):
+            pltpu.make_async_remote_copy(
+                packed.at[rows_of(rank)], packed.at[rows_of(rank)], sum_ssem, sum_rsem,
+                device_id=offset_device(me, i + 1, 1), device_id_type=MESH,
+            ).start()
+
+        loop(DEVICES - 1, send_sum)
+        both_ends(packed.at[pl.ds(0, (OWNERS - 1) * PIECE)], sum_ssem, sum_rsem).wait_recv()
+        both_ends(partial.at[pl.ds(0, (OWNERS - 1) * PIECE)], part_ssem, part_rsem).wait_send()
+        both_ends(pieces.at[pl.ds(1, DEVICES - 1)], sum_ssem, sum_rsem).wait_send()
+
+    @pl.when(jnp.logical_not(owns))
+    def _():
+        both_ends(packed.at[pl.ds(0, OWNERS * PIECE)], sum_ssem, sum_rsem).wait_recv()
+        both_ends(partial.at[pl.ds(0, OWNERS * PIECE)], part_ssem, part_rsem).wait_send()
+
+    result = pltpu.make_async_copy(packed, packed_hbm, misc_sem.at[0])
+    result.start()
+
     sent = flux_out.at[pl.ds(ROWS, (DEVICES - 1) * ROWS)]
     pltpu.make_async_remote_copy(
         sent, sent, flux_ssem, flux_rsem.at[0], device_id=offset_device(me, 1, 1), device_id_type=MESH
@@ -381,6 +490,39 @@
         sent, sent, back_ssem, back_rsem.at[0], device_id=offset_device(me, 1, 1), device_id_type=MESH
     ).wait_send()
     store.wait()
+    result.wait()
+
+
+def finish(
+    inv, anew_in, onew_arr, packed, anew, onew, gtaps, gagain, gup, gdown, gcouple, gogain, goup, godown
+):
+    part = onew.shape[0]
+    first = pl.program_id(0) * part
+
+    def place(i):
+        for j in range(8):
+            onew[i * 8 + j] = onew_arr[inv[0, first + i * 8 + j] & 255]
+
+    loop(part // 8, place)
+
+    @pl.when(pl.program_id(0) == 0)
+    def _():
+        anew[...] = anew_in[...]
+        goup[:, 0:128] = packed[AT_OUP : AT_OUP + 128, :].astype(F32)
+        goup[:, 128:256] = packed[AT_OUP + 128 : AT_OUP + 256, :].astype(F32)
+        godown[...] = packed[AT_ODOWN : AT_ODOWN + 256, :].astype(F32)
+        gcouple[...] = packed[AT_COUPLE : AT_COUPLE + 256, :].astype(F32)
+        small = packed[AT_SMALL : AT_SMALL + 32, :].astype(F32)
+        for a in range(3):
+            for i in range(2):
+                gtaps[a, :, 128 * i : 128 * (i + 1)] = small[9 * i + 3 * a : 9 * i + 3 * a + 3]
+        gagain[:, 0:128] = small[18:19]
+        gagain[:, 128:256] = small[19:20]
+        gogain[...] = small[20:21]
+        for i in range(2):
+            gdown[:, 128 * i : 128 * (i + 1)] = packed[AT_DOWN + 512 * i : AT_DOWN + 512 * (i + 1), :].astype(F32)
+        for i in range(4):
+            gup[:, 128 * i : 128 * (i + 1)] = packed[AT_UP + 256 * i : AT_UP + 256 * (i + 1), :].astype(F32)
 
 
 def body(
@@ -390,56 +532,20 @@
     height, breadth, channels = atm_state.shape
     blocks = ocean_state.shape[0]
     n_rows = blocks * 32
-
-    target = owner_slot // blocks
-    mine = digits(lax.axis_index("tx"), lax.axis_index("ty"))
-    theirs = digits(target // 16, target % 16)
-    dx, dy, dz, dc = [(t - m) % n for t, m, n in zip(theirs, mine, (4, 4, 4, 2))]
-    step = ((((dz * 4 + dy) * 4 + dx) * 2 + dc) * UNMIX) % DEVICES
-    index = jnp.arange(blocks, dtype=I32)
-    earlier = (target[:, None] == target[None, :]) & (index[:, None] < index[None, :])
-    place = 2 * step + jnp.sum(earlier.astype(I32), axis=0)
-    order = (place[None, :] == index[:, None]).astype(F32)
-    shares = margin_area / jnp.sum(margin_area, axis=1, keepdims=True)
-    table = jnp.concatenate(
-        [
-            margin_cell.reshape(blocks, -1).astype(F32),
-            shares.reshape(blocks, -1),
-            (owner_slot % blocks).astype(F32)[:, None],
-        ],
-        axis=1,
-    )
-    table = jnp.dot(order, table, precision=lax.Precision.HIGHEST, preferred_element_type=F32)
-    cells = jnp.round(table[:, :128]).astype(I32).reshape(blocks, 4, 32).transpose(1, 0, 2).reshape(4, n_rows)
-    shares = table[:, 128:256].reshape(blocks, 4, 32).transpose(1, 0, 2).reshape(4, n_rows)
-    slots = jnp.round(table[:, 256]).astype(I32).reshape(DEVICES, 1, 2)
-    slots = jnp.pad(slots, ((0, 0), (0, 0), (0, 126)))
-
+    n_cells = height * breadth
     vmem, any_ = pl.BlockSpec(memory_space=pltpu.VMEM), pl.BlockSpec(memory_space=pl.ANY)
-    out_shape = [
-        jax.ShapeDtypeStruct((height, breadth, channels), BF16),
-        jax.ShapeDtypeStruct((blocks, 32, 128), BF16),
-        jax.ShapeDtypeStruct((9, 256), F32),
-        jax.ShapeDtypeStruct((1, 256), F32),
-        jax.ShapeDtypeStruct((256, 512), F32),
-        jax.ShapeDtypeStruct((512, 256), F32),
-        jax.ShapeDtypeStruct((256, 128), F32),
-        jax.ShapeDtypeStruct((1, 128), F32),
-        jax.ShapeDtypeStruct((128, 256), F32),
-        jax.ShapeDtypeStruct((256, 128), F32),
-    ]
     block = lambda: pltpu.VMEM((blocks, 32, 128), BF16)
     flat = lambda: pltpu.VMEM((n_rows, 128), BF16)
-    n_cells = height * breadth
     scratch = [
         block(), block(), block(),
+        pltpu.VMEM((4, blocks // 4, 128), I32),
+        pltpu.VMEM((4, blocks // 4, 128), F32),
         pltpu.VMEM((n_cells, n_rows), BF16),
         flat(), flat(), flat(), flat(),
-        block(), block(),
-        pltpu.VMEM((DEVICES, 1, 128), I32),
-        pltpu.VMEM((8, 256), I32),
-        pltpu.SMEM((DEVICES, 1, 128), I32),
-        pltpu.SMEM((8, 256), I32),
+        block(),
+        pltpu.VMEM((DEVICES, 128), I32),
+        pltpu.VMEM((DEVICES, 128), I32),
+        pltpu.SMEM((DEVICES, 128), I32),
         pltpu.VMEM((height + 2, breadth + 16, channels), F32),
         pltpu.VMEM((n_cells, 256), F32),
         pltpu.VMEM((n_cells, 128), F32),
@@ -448,6 +554,17 @@
         pltpu.VMEM((n_cells, 512), BF16),
         pltpu.VMEM((n_cells, 128), BF16),
         pltpu.VMEM((n_cells, 256), F32),
+        pltpu.VMEM((16, 256), F32),
+        pltpu.VMEM((1, 256), F32),
+        pltpu.VMEM((256, 512), F32),
+        pltpu.VMEM((512, 256), F32),
+        pltpu.VMEM((1, 128), F32),
+        pltpu.VMEM((128, 256), F32),
+        pltpu.VMEM((256, 128), F32),
+        pltpu.VMEM((32, 128), F32),
+        pltpu.VMEM((PACKED, 128), BF16),
+        pltpu.VMEM((DEVICES, PIECE, 128), BF16),
+        pltpu.VMEM((PACKED, 128), BF16),
         pltpu.VMEM((16, channels), BF16),
         pltpu.VMEM((16, channels), BF16),
         pltpu.VMEM((breadth, channels), BF16),
@@ -462,26 +579,61 @@
         pltpu.SemaphoreType.DMA((GROUPS,)),
         pltpu.SemaphoreType.DMA,
         pltpu.SemaphoreType.DMA((GROUPS,)),
-        pltpu.SemaphoreType.DMA((3,)),
+        pltpu.SemaphoreType.DMA((2,)),
+        pltpu.SemaphoreType.DMA,
+        pltpu.SemaphoreType.DMA,
+        pltpu.SemaphoreType.DMA,
+        pltpu.SemaphoreType.DMA,
     ]
-    anew, onew, gtaps, *grads = pl.pallas_call(
+    anew, onew_arr, inv, packed = pl.pallas_call(
         kernel,
-        out_shape=out_shape,
+        out_shape=[
+            jax.ShapeDtypeStruct((height, breadth, channels), BF16),
+            jax.ShapeDtypeStruct((blocks, 32, 128), BF16),
+            jax.ShapeDtypeStruct((8, 256), I32),
+            jax.ShapeDtypeStruct((PACKED, 128), BF16),
+        ],
         in_specs=[vmem] * 14 + [any_] * 2,
-        out_specs=[vmem, any_] + [vmem] * 8,
+        out_specs=[vmem, any_, vmem, any_],
         scratch_shapes=scratch,
         compiler_params=pltpu.CompilerParams(
             collective_id=0, has_side_effects=True, vmem_limit_bytes=56 * 1024 * 1024
         ),
     )(
-        atm_state, kernel_taps.reshape(9, channels), atm_gain.reshape(1, -1), atm_up, atm_down, couple_weight,
-        ocean_gain.reshape(1, -1), ocean_up, ocean_down, land_mask, cells, shares, slots,
-        atm_cotangent, ocean_state, ocean_cotangent,
+        atm_state, kernel_taps, atm_gain.reshape(1, -1), atm_up, atm_down, couple_weight,
+        ocean_gain.reshape(1, -1), ocean_up, ocean_down, land_mask.T, margin_cell.transpose(1, 2, 0),
+        margin_area.transpose(1, 2, 0), owner_slot.reshape(1, -1), atm_cotangent, ocean_state, ocean_cotangent,
     )
-    sums = lax.psum((gtaps, *grads), ("tx", "ty"))
+    part = blocks // 4
+    whole = lambda *shape: pl.BlockSpec(shape, lambda i: (0,) * len(shape))
+    anew, onew, gtaps, gagain, gup, gdown, gcouple, gogain, goup, godown = pl.pallas_call(
+        finish,
+        grid=(4,),
+        out_shape=[
+            jax.ShapeDtypeStruct((height, breadth, channels), BF16),
+            jax.ShapeDtypeStruct((blocks, 32, 128), BF16),
+            jax.ShapeDtypeStruct((3, 3, 256), F32),
+            jax.ShapeDtypeStruct((1, 256), F32),
+            jax.ShapeDtypeStruct((256, 512), F32),
+            jax.ShapeDtypeStruct((512, 256), F32),
+            jax.ShapeDtypeStruct((256, 128), F32),
+            jax.ShapeDtypeStruct((1, 128), F32),
+            jax.ShapeDtypeStruct((128, 256), F32),
+            jax.ShapeDtypeStruct((256, 128), F32),
+        ],
+        in_specs=[
+            pl.BlockSpec(memory_space=pltpu.SMEM),
+            whole(height, breadth, channels), whole(blocks, 32, 128), whole(PACKED, 128),
+        ],
+        out_specs=[
+            whole(height, breadth, channels), pl.BlockSpec((part, 32, 128), lambda i: (i, 0, 0)), whole(3, 3, 256),
+            whole(1, 256), whole(256, 512), whole(512, 256), whole(256, 128), whole(1, 128), whole(128, 256),
+            whole(256, 128),
+        ],
+        compiler_params=pltpu.CompilerParams(vmem_limit_bytes=40 * 1024 * 1024),
+    )(inv, anew, onew_arr, packed)
     return (
-        anew, onew, sums[0].reshape(3, 3, channels), sums[1].reshape(-1), sums[2], sums[3], sums[4],
-        sums[5].reshape(-1), sums[6], sums[7],
+        anew, onew, gtaps, gagain.reshape(-1), gup, gdown, gcouple, gogain.reshape(-1), goup, godown,
     )
 
 

time: 275 us -> 140 us (0.51)
  waiting for transfers between devices: 81.5 us -> 0 us
  blocking collectives: 67 us -> 0 us
  Pallas kernels: 92.6 us -> 134 us
  between operations: 14.2 us -> 0.67 us
  local copies, waits for them, and re-layouts: 15.2 us -> 4.34 us
  other arithmetic: 3.66 us -> 0 us
    psum x1 -> x0, waiting for transfers between devices: 81.5 us -> none  [body(): sums = lax.psum((gtaps, *grads), ('tx', 'ty'))]
    psum x1 -> x0, blocking collectives: 67 us -> none  [body(): sums = lax.psum((gtaps, *grads), ('tx', 'ty'))]
    pallas_call x1 -> x2, Pallas kernels: 92.6 us -> 134 us  [the longest x1 131 us: body(): pl.pallas_call(kernel, out_shape=[jax.ShapeDtypeStruct((height, breadth,...]
    unnamed x18 -> x8, local copies, waits for them, and re-layouts: 10.1 us -> 4.34 us
    reshape x6 -> x0, local copies, waits for them, and re-layouts: 4.28 us -> none  [the longest x1 1.32 us: body(): kernel_taps.reshape(9, channels)]
  transfers between devices with their start and end apart: 1 -> 0, of which waited for: 1 -> 0; matrix products, arithmetic and copies ran while one was open for 0% -> 0% of each run, Pallas kernels for 0% -> 0%
where the time goes in v2:
time: 140 us; the launch traced here: 139 us
  Pallas kernels  134 us (96%)
  local copies, waits for them, and re-layouts  4.34 us (3%)
    pallas_call x1, Pallas kernels, body(): pl.pallas_call(kernel, out_shape=[jax.ShapeDtypeStruct((height, breadth,...  131 us
    unnamed x8, local copies, waits for them, and re-layouts  4.34 us
    pallas_call x1, Pallas kernels, body(): pl.pallas_call(finish, grid=(4,), out_shape=[jax.ShapeDtypeStruct((height...  3.62 us

profile of v2, /device:TPU:1, one launch (start us, length us, event | category | flops | bytes accessed | tf_op | source)
XLA Modules:
  0.0 139.3 jit_solution(3996305309755413799)
XLA Ops:
  0.6 130.7 %shard_map.231 = (bf16[8,64,256]{2,1,0:T(8,128)(2,1)}, bf16[256,32,128]{2,1,0:T(8,128)(2,1)}, s32[8,256]{1,0:T(8,128)}, bf16[2848,128]{1,0:T(8,128)(2,1)}) custom-call(bf16[8,64,256]{2,1,0:T(8,128)(2,1)} %atm.1, f32[3,3,256]{2,1,0:T(4,128)} %taps.1, f32[1,256]{1,0:T(1,128)} %bitcast.11, bf16[256,512]{1,0:T(8,128)(2,1)} %up.1, bf16[512,256]{1,0:T(8,128)(2,1)} %down.1, ...), custom_call_target="tpu_custom_call" | custom-call | tf_op jit(solution)/shard_map/pallas_call | solution.py:588
  131.3 0.0 copy-start
  131.4 1.6 %copy-done = bf16[256,32,128]{2,1,0:T(8,128)(2,1)S(1)} copy-done((bf16[256,32,128]{2,1,0:T(8,128)(2,1)S(1)}, bf16[256,32,128]{2,1,0:T(8,128)(2,1)}, u32[]{:S(2)}) %copy-start) | copy-done | bytes 2097176
  132.9 0.0 copy-start.1
  132.9 1.1 copy-done.1
  134.1 0.0 copy-start.2
  134.1 0.9 copy-done.2
  135.0 0.0 copy-start.3
  135.0 0.7 copy-done.3
  135.7 3.6 %shard_map.232 = (bf16[8,64,256]{2,1,0:T(8,128)(2,1)}, bf16[256,32,128]{2,1,0:T(8,128)(2,1)}, f32[3,3,256]{2,1,0:T(4,128)}, f32[1,256]{1,0:T(1,128)}, f32[256,51...) custom-call(s32[8,256]{1,0:T(8,128)S(1)} %copy-done.3, ...), custom_call_target="tpu_custom_call" | custom-call | tf_op jit(solution)/shard_map/pallas_call | solution.py:609
Async XLA Ops:
  131.3 1.6 %copy-start = (bf16[256,32,128]{2,1,0:T(8,128)(2,1)S(1)}, bf16[256,32,128]{2,1,0:T(8,128)(2,1)}, u32[]{:S(2)}) copy-start(bf16[256,32,128]{2,1,0:T(8,128)(2,1)} %get-tuple-element.26.onew_arr) | copy-start | bytes 6291460
  132.9 1.1 copy-start.1
  134.1 0.9 copy-start.2
  135.0 0.7 copy-start.3

commit v3 on v2

v3 whole, which is shorter than its diff:
```python
import functools

import jax
import jax.numpy as jnp
from jax import lax
from jax.experimental import pallas as pl
from jax.experimental.pallas import tpu as pltpu
from jax.sharding import PartitionSpec as P

EPS = 1e-06
MESH = pl.DeviceIdType.MESH
F32, BF16, I32 = jnp.float32, jnp.bfloat16, jnp.int32
DEVICES = 128
MIX = 37
UNMIX = pow(MIX, -1, DEVICES)
ROWS = 64
GROUP = 8
GROUPS = DEVICES // GROUP
PIECE = 16
LATE = DEVICES * PIECE
EARLY = 768
HALF, QUARTER = EARLY // 2, EARLY // 8


def digits(tx, ty):
    return (tx // 4) * 2 + ty // 8, (ty // 2) % 4, tx % 4, ty % 2


def rem(a, n):
    return lax.rem(a, jnp.int32(n))


def div(a, n):
    return lax.div(a, jnp.int32(n))


def device(x, y, z, c):
    return (div(x, 2) * 4 + z, rem(x, 2) * 8 + y * 2 + c)


def offset_device(me, step, sign):
    code = rem(step * MIX, DEVICES)
    x = rem(me[0] + 4 + sign * rem(div(code, 2), 4), 4)
    y = rem(me[1] + 4 + sign * rem(div(code, 8), 4), 4)
    z = rem(me[2] + 4 + sign * div(code, 32), 4)
    return device(x, y, z, rem(me[3] + code, 2))


def rank_of(tx, ty):
    return rem((tx * 16 + ty) * MIX, DEVICES)


def sigmoid(v):
    return 0.5 * jnp.tanh(0.5 * v) + 0.5


def dot(a, b):
    return jnp.dot(a, b, preferred_element_type=F32)


def dot_t(a, b):
    return lax.dot_general(a, b, (((1,), (1,)), ((), ())), preferred_element_type=F32)


def t_dot(a, b):
    return lax.dot_general(a, b, (((0,), (0,)), ((), ())), preferred_element_type=F32)


def loop(n, f):
    lax.fori_loop(0, n, lambda i, c: (f(i), c)[1], 0)


def kernel(
    atm, taps, again, up, down, couple, ogain, oup, odown, mask, margin_cell, margin_area, owner, acot, ostate_hbm, ocot_hbm,
    anew, onew_hbm, inv_v, late_hbm, early_hbm, small_hbm,
    ostate, ocot, wet, cells, shares, spread, flux_out, flux_in, back_out, back_in, onew_arr, owners, slots_v, slots_s,
    win, unit, inv_rms, normed, pre, act, gather, coupled_t, sgrad, up_t, down_t, couple_t, oup_t, odown_t,
    gtaps, gagain, gup, gdown_t, gogain, goup, godown_t, small, late, pieces, late_sum,
    early, early_core, early_mine, early_x, early_y, early_z, early_sum, small_core, small_x, small_y, small_z,
    edge_w, edge_e, halo_n, halo_s, halo_c,
    load_sem, halo_ssem, halo_rsem, own_ssem, own_rsem, flux_ssem, flux_rsem, back_ssem, back_rsem, misc_sem,
    late_ssem, late_rsem, sum_ssem, sum_rsem, early_ssem, early_rsem, small_ssem, small_rsem,
):
    tx, ty = lax.axis_index("tx"), lax.axis_index("ty")
    me = digits(tx, ty)
    height, breadth = atm.shape[0], atm.shape[1]
    n_cells = height * breadth

    barrier = pltpu.get_barrier_semaphore()
    loads = [
        pltpu.make_async_copy(ostate_hbm, ostate, load_sem.at[0]),
        pltpu.make_async_copy(ocot_hbm, ocot, load_sem.at[1]),
    ]
    for load in loads:
        load.start()

    xs = [rem(me[0] + i, 4) for i in range(4)]
    ys = [rem(me[1] + i, 4) for i in range(4)]
    zs = [rem(me[2] + i, 4) for i in range(4)]
    cs = [me[3], 1 - me[3]]
    for i in range(1, DEVICES):
        pl.semaphore_signal(
            barrier, inc=1, device_id=device(xs[i // 2 % 4], ys[i // 8 % 4], zs[i // 32], cs[i % 2]), device_id_type=MESH
        )
    partner = device(xs[0], ys[0], zs[0], cs[1])
    x_peers = [device(xs[i], ys[0], zs[0], cs[0]) for i in (1, 3, 2)]
    y_peers = [device(xs[0], ys[i], zs[0], cs[0]) for i in (1, 3, 2)]
    z_peers = [device(xs[0], ys[0], zs[i], cs[0]) for i in (1, 3, 2)]

    def remote(src, dst, ssem, rsem, to):
        return pltpu.make_async_remote_copy(src, dst, ssem, rsem, device_id=to, device_id_type=MESH)

    def both_ends(ref, ssem, rsem):
        return remote(ref, ref, ssem, rsem, partner)

    edge_w[...] = jnp.zeros_like(edge_w)
    edge_e[...] = jnp.zeros_like(edge_e)

    def own_rows(y):
        win[y + 1, 8 : 8 + breadth, :] = atm[y].astype(F32)

    loop(height, own_rows)
    west = jnp.concatenate([win[y + 1, 8:9, :] for y in range(height)], axis=0)
    east = jnp.concatenate([win[y + 1, 7 + breadth : 8 + breadth, :] for y in range(height)], axis=0)
    nothing = jnp.zeros_like(west)
    edge_w[...] = jnp.concatenate([west, nothing], axis=0).astype(BF16)
    edge_e[...] = jnp.concatenate([east, nothing], axis=0).astype(BF16)

    pl.semaphore_wait(barrier, DEVICES - 1)

    te, tw = (tx + 1) % 8, (tx + 7) % 8
    north, south = ty > 0, ty < 15

    def halo(i, src, dst, dx, dy):
        return pltpu.make_async_remote_copy(
            src, dst, halo_ssem.at[i], halo_rsem.at[i], device_id=(dx, dy), device_id_type=MESH
        )

    copies = [
        (south, halo(0, atm.at[height - 1], halo_n, tx, (ty + 1) % 16)),
        (north, halo(1, atm.at[0], halo_s, tx, (ty + 15) % 16)),
        (None, halo(2, edge_e, halo_c.at[0], te, ty)),
        (None, halo(3, edge_w, halo_c.at[1], tw, ty)),
        (south, halo(4, edge_e, halo_c.at[2], te, (ty + 1) % 16)),
        (south, halo(5, edge_w, halo_c.at[3], tw, (ty + 1) % 16)),
        (north, halo(6, edge_e, halo_c.at[4], te, (ty + 15) % 16)),
        (north, halo(7, edge_w, halo_c.at[5], tw, (ty + 15) % 16)),
    ]

    def when(cond, f):
        if cond is None:
            f()
        else:
            pl.when(cond)(f)

    for cond, copy in copies:
        when(cond, copy.start)

    owners[0:1, :] = owner[...]

    def own_phase(i, rows, peers):
        for n, to in zip((1, 3, 2), peers):
            remote(
                owners.at[pl.ds(0, rows)], owners.at[pl.ds(n * rows, rows)], own_ssem.at[i], own_rsem.at[i], to
            ).start()

    def own_wait(i, rows, peers):
        both_ends(owners.at[pl.ds(rows, rows * peers)], own_ssem.at[i], own_rsem.at[i]).wait_recv()

    own_phase(0, 1, [partner])

    slot = owner[...]
    t_tx, t_ty = slot >> 12, (slot >> 8) & 15
    theirs = ((t_tx >> 2) * 2 + (t_ty >> 3), (t_ty >> 1) & 3, t_tx & 3, t_ty & 1)
    dx, dy, dz, dc = [(t - m + n) & (n - 1) for t, m, n in zip(theirs, me, (4, 4, 4, 2))]
    step = ((((dz * 4 + dy) * 4 + dx) * 2 + dc) * UNMIX) & (DEVICES - 1)
    blocks = slot.shape[1]
    square = jnp.broadcast_to(step, (blocks, blocks))
    first = lax.broadcasted_iota(I32, square.shape, 0)
    second = lax.broadcasted_iota(I32, square.shape, 1)
    same = (square.astype(F32).T == square.astype(F32)) & (first < second)
    place = 2 * step + jnp.sum(same.astype(F32), axis=0, keepdims=True).astype(I32)

    area = margin_area[...]
    share = (area / jnp.sum(area, axis=0, keepdims=True)).reshape(128, blocks).astype(BF16)
    cell = margin_cell[...].reshape(128, blocks)
    high, low = (cell >> 4).astype(F32).astype(BF16), (cell & 15).astype(F32).astype(BF16)
    quads = lax.broadcasted_iota(I32, (blocks // 4, blocks), 0)
    lane_block = lax.broadcasted_iota(I32, (blocks // 4, 128), 1) // 32
    got_share = [jnp.zeros((blocks // 4, 128), F32)] * 4
    got_cell = [jnp.zeros((blocks // 4, 128), F32)] * 4
    for j in range(4):
        pick = (place == 4 * quads + j).astype(F32).astype(BF16)
        one_share = dot_t(pick, share)
        one_cell = 16.0 * dot_t(pick, high) + dot_t(pick, low)
        for k in range(4):
            turn = (32 * (j - k)) % 128
            here = lane_block == j
            got_share[k] = jnp.where(here, pltpu.roll(one_share, turn, 1) if turn else one_share, got_share[k])
            got_cell[k] = jnp.where(here, pltpu.roll(one_cell, turn, 1) if turn else one_cell, got_cell[k])
    for k in range(4):
        shares[k] = got_share[k]
        cells[k] = got_cell[k].astype(I32)

    for weight, turned in ((up, up_t), (down, down_t), (couple, couple_t), (oup, oup_t), (odown, odown_t)):
        turned[...] = weight[...].astype(F32).T.astype(BF16)

    own_wait(0, 1, 1)
    own_phase(1, 2, x_peers)

    for cond, copy in copies:
        when(cond, copy.wait_send)
    receives = [north, south, None, None, north, north, south, south]
    for cond, (_, copy) in zip(receives, copies):
        when(cond, copy.wait_recv)

    @pl.when(north)
    def _():
        win[0, 8 : 8 + breadth, :] = halo_n[...].astype(F32)
        win[0, 7:8, :] = halo_c[2].astype(F32)[height - 1 : height]
        win[0, 8 + breadth : 9 + breadth, :] = halo_c[3].astype(F32)[height - 1 : height]

    @pl.when(jnp.logical_not(north))
    def _():
        win[0] = jnp.zeros(win.shape[1:], F32)

    @pl.when(south)
    def _():
        win[height + 1, 8 : 8 + breadth, :] = halo_s[...].astype(F32)
        win[height + 1, 7:8, :] = halo_c[4].astype(F32)[0:1]
        win[height + 1, 8 + breadth : 9 + breadth, :] = halo_c[5].astype(F32)[0:1]

    @pl.when(jnp.logical_not(south))
    def _():
        win[height + 1] = jnp.zeros(win.shape[1:], F32)

    west, east = halo_c[0].astype(F32), halo_c[1].astype(F32)
    for y in range(height):
        win[y + 1, 7:8, :] = west[y : y + 1]
        win[y + 1, 8 + breadth : 9 + breadth, :] = east[y : y + 1]

    def stencil_row(y):
        total = jnp.zeros((breadth, 256), F32)
        for a in range(3):
            for b in range(3):
                total = total + taps[a, b : b + 1, :] * win[y + a, 7 + b : 7 + b + breadth, :]
        inv = lax.rsqrt(jnp.mean(total * total, axis=-1, keepdims=True) + EPS)
        here = pl.ds(pl.multiple_of(y * breadth, breadth), breadth)
        u = total * inv
        unit[here, :] = u
        inv_rms[here, :] = jnp.broadcast_to(inv, (breadth, 128))
        normed[here, :] = (u * again[...]).astype(BF16)

    loop(height, stencil_row)
    own_wait(1, 2, 3)
    own_phase(2, 8, y_peers)

    def atm_mlp(i):
        here = pl.ds(pl.multiple_of(i * 128, 128), 128)
        v = dot(normed[here, :], up[...])
        pre[here, :] = v
        a = (v * sigmoid(v)).astype(BF16)
        act[here, :] = a
        old = atm[pl.ds(i * 2, 2)].reshape(128, 256).astype(F32)
        anew[pl.ds(i * 2, 2)] = (old + dot(a, down[...])).astype(BF16).reshape(2, breadth, 256)

    loop(4, atm_mlp)
    coupled_t[...] = dot_t(couple_t[...], anew[...].reshape(n_cells, 256)).astype(BF16)
    own_wait(2, 8, 3)
    own_phase(3, 32, z_peers)

    def spread_columns(i):
        here = pl.ds(pl.multiple_of(i * 128, 128), 128)
        rows = lax.broadcasted_iota(I32, (n_cells, 128), 0)
        row = pl.ds(i, 1)
        total = jnp.where(rows == cells[0, row, :], shares[0, row, :], 0.0)
        for k in range(1, 4):
            total = total + jnp.where(rows == cells[k, row, :], shares[k, row, :], 0.0)
        spread[:, here] = total.astype(BF16)

    def flux_copy(step, sign):
        here = pl.ds(pl.multiple_of(step * ROWS, ROWS), ROWS)
        return pltpu.make_async_remote_copy(
            flux_out.at[here], flux_in.at[here], flux_ssem, flux_rsem.at[step // GROUP],
            device_id=offset_device(me, step, sign), device_id_type=MESH,
        )

    def flux_group(g):
        for j in range(GROUP // 2):
            spread_columns(g * (GROUP // 2) + j)
        here = pl.ds(pl.multiple_of(g * (GROUP * ROWS), GROUP * ROWS), GROUP * ROWS)
        flux_out[here, :] = dot(coupled_t[...], spread[:, here]).astype(BF16).T
        pl.when(g > 0)(lambda: flux_copy(g * GROUP, 1).start())
        for j in range(1, GROUP):
            flux_copy(g * GROUP + j, 1).start()

    loop(GROUPS, flux_group)
    flux_in[0:ROWS, :] = flux_out[0:ROWS, :]

    ones = jnp.ones((32, 128), BF16)
    wet_rows_of = mask[...].astype(F32).astype(BF16)

    def wet_rows(i):
        rows = lax.broadcasted_iota(I32, (512, blocks), 0)
        cols = lax.broadcasted_iota(I32, (512, blocks), 1)
        pick = (rows // 32 + i * 16 == cols).astype(F32).astype(BF16)
        wide = dot_t(pick, wet_rows_of)
        r2 = lax.broadcasted_iota(I32, wide.shape, 0)
        c2 = lax.broadcasted_iota(I32, wide.shape, 1)
        wide = jnp.where(r2 % 32 == c2, wide, 0.0).astype(BF16)
        wet[pl.ds(pl.multiple_of(i * 16, 16), 16)] = dot(wide, ones).astype(BF16).reshape(16, 32, 128)

    loop(16, wet_rows)

    own_wait(3, 32, 3)
    owned = owners[...]
    lane = lax.broadcasted_iota(I32, owned.shape, 1)
    hit = (owned >> 8) == tx * 16 + ty
    lane_f = lane.astype(F32)
    local = (owned & (blocks - 1)).astype(F32)
    one = jnp.min(jnp.where(hit, lane_f, 1e4), axis=1, keepdims=True)
    two = jnp.max(jnp.where(hit, lane_f, -1.0), axis=1, keepdims=True)
    one = jnp.sum(jnp.where(lane_f == one, local, 0.0), axis=1, keepdims=True).astype(I32)
    two = jnp.sum(jnp.where(lane_f == two, local, 0.0), axis=1, keepdims=True).astype(I32)
    position = 2 * ((lax.broadcasted_iota(I32, owned.shape, 0) * UNMIX) & (DEVICES - 1))
    found = jnp.where(one == lane, position, 0) + jnp.where(two == lane, position + 1, 0)
    inv_v[...] = jnp.broadcast_to(
        jnp.max(found.astype(F32), axis=0, keepdims=True).astype(I32), inv_v.shape
    )
    slots_v[...] = jnp.where(lane[:, 0:128] == 0, one, two)
    to_scalar = pltpu.make_async_copy(slots_v, slots_s, misc_sem.at[0])
    to_scalar.start()
    to_scalar.wait()
    for load in loads:
        load.wait()

    goup[...] = jnp.zeros_like(goup)
    godown_t[...] = jnp.zeros_like(godown_t)
    gogain[...] = jnp.zeros_like(gogain)

    def back_copy(step, sign):
        here = pl.ds(pl.multiple_of(step * ROWS, ROWS), ROWS)
        return pltpu.make_async_remote_copy(
            back_out.at[here], back_in.at[here], back_ssem, back_rsem.at[step // GROUP],
            device_id=offset_device(me, step, sign), device_id_type=MESH,
        )

    def wait_group(g, buf, ssem, rsem):
        def first():
            some = buf.at[pl.ds(ROWS, (GROUP - 1) * ROWS)]
            pltpu.make_async_remote_copy(
                some, some, ssem, rsem.at[0], device_id=offset_device(me, 1, 1), device_id_type=MESH
            ).wait_recv()

        def later():
            some = buf.at[pl.ds(pl.multiple_of(g * (GROUP * ROWS), GROUP * ROWS), GROUP * ROWS)]
            pltpu.make_async_remote_copy(
                some, some, ssem, rsem.at[g], device_id=offset_device(me, 1, 1), device_id_type=MESH
            ).wait_recv()

        pl.when(g == 0)(first)
        pl.when(g > 0)(later)

    def ocean_group(g):
        wait_group(g, flux_in, flux_ssem, flux_rsem)
        here = pl.ds(pl.multiple_of(g * (GROUP * ROWS), GROUP * ROWS), GROUP * ROWS)
        codes = [rem((g * GROUP + j) * MIX, DEVICES) for j in range(GROUP)]
        slot = [slots_s[codes[j // 2], j % 2] & 255 for j in range(2 * GROUP)]
        state = jnp.concatenate([ostate[s] for s in slot], axis=0).astype(F32)
        wets = jnp.concatenate([wet[s] for s in slot], axis=0)
        out_grad = jnp.concatenate([ocot[s] for s in slot], axis=0) * wets
        total = state + flux_in[here, :].astype(F32)
        inv = lax.rsqrt(jnp.mean(total * total, axis=-1, keepdims=True) + EPS)
        u = total * inv
        nrm = (u * ogain[...]).astype(BF16)
        v = dot(nrm, oup[...])
        s = sigmoid(v)
        a = (v * s).astype(BF16)
        onew_arr[pl.ds(g * (2 * GROUP), 2 * GROUP)] = (
            (state + wets.astype(F32) * dot(a, odown[...])).astype(BF16).reshape(2 * GROUP, 32, 128)
        )
        godown_t[...] += t_dot(out_grad, a)
        pg = (dot(out_grad, odown_t[...]) * (s * (1.0 + v * (1.0 - s)))).astype(BF16)
        goup[...] += t_dot(nrm, pg)
        ng = dot(pg, oup_t[...])
        gogain[...] += jnp.sum(ng * u, axis=0, keepdims=True)
        gg = ng * ogain[...]
        tg = inv * (gg - u * jnp.mean(gg * u, axis=-1, keepdims=True))
        back_out[here, :] = tg.astype(BF16)

        pl.when(g > 0)(lambda: back_copy(g * GROUP, -1).start())
        for j in range(1, GROUP):
            back_copy(g * GROUP + j, -1).start()

    loop(GROUPS, ocean_group)
    back_in[0:ROWS, :] = back_out[0:ROWS, :]

    store = pltpu.make_async_copy(onew_arr, onew_hbm, misc_sem.at[1])
    store.start()
    for i in range(2):
        early[128 * i : 128 * (i + 1), :] = goup[:, 128 * i : 128 * (i + 1)].astype(BF16)
        early[256 + 128 * i : 256 + 128 * (i + 1), :] = godown_t[:, 128 * i : 128 * (i + 1)].astype(BF16)

    sgrad[:, 0:128] = jnp.zeros((n_cells, 128), F32)

    def back_group(g):
        wait_group(g, back_in, back_ssem, back_rsem)
        here = pl.ds(pl.multiple_of(g * (GROUP * ROWS), GROUP * ROWS), GROUP * ROWS)
        sgrad[:, 0:128] += dot(spread[:, here], back_in[here, :])

    loop(GROUPS, back_group)
    gathered = sgrad[:, 0:128].astype(BF16)
    gather[...] = gathered
    gcouple_t = t_dot(gathered, anew[...].reshape(n_cells, 256)).astype(BF16)
    for i in range(2):
        early[512 + 128 * i : 512 + 128 * (i + 1), :] = gcouple_t[:, 128 * i : 128 * (i + 1)]

    x, y, z, c = me

    def span(i, n):
        return pl.ds(pl.multiple_of(i * n, n), n)

    def early_copy(i, src, dst, to):
        remote(src, dst, early_ssem.at[i], early_rsem.at[i], to).start()

    def early_wait(i, ref):
        both_ends(ref, early_ssem.at[i], early_rsem.at[i]).wait_recv()

    def add_four(ref):
        rows = ref.shape[0] // 4
        total = ref[0:rows, :]
        for i in range(1, 4):
            total = total + ref[i * rows : (i + 1) * rows, :]
        return total

    def early_0():
        early_copy(0, early.at[span(1 - c, HALF)], early_core, partner)

    def early_1():
        early_wait(0, early_core)
        early_mine[...] = early[span(c, HALF), :].astype(F32) + early_core[...].astype(F32)
        early_x[span(x, QUARTER), :] = early_mine[span(x, QUARTER), :]
        for n, to in zip((1, 3, 2), x_peers):
            early_copy(1, early_mine.at[span(xs[n], QUARTER)], early_x.at[span(x, QUARTER)], to)

    def early_2():
        early_wait(1, early_x.at[pl.ds(0, 3 * QUARTER)])
        early_y[span(y, QUARTER), :] = add_four(early_x)
        for to in y_peers:
            early_copy(2, early_y.at[span(y, QUARTER)], early_y.at[span(y, QUARTER)], to)

    def early_3():
        early_wait(2, early_y.at[pl.ds(0, 3 * QUARTER)])
        early_z[span(z, QUARTER), :] = add_four(early_y)
        for to in z_peers:
            early_copy(3, early_z.at[span(z, QUARTER)], early_z.at[span(z, QUARTER)], to)

    def early_4():
        early_wait(3, early_z.at[pl.ds(0, 3 * QUARTER)])
        here = span(c * 4 + x, QUARTER)
        early_sum[here, :] = add_four(early_z).astype(BF16)
        for to in x_peers:
            early_copy(4, early_sum.at[here], early_sum.at[here], to)

    def early_5():
        early_wait(4, early_sum.at[pl.ds(0, 3 * QUARTER)])
        here = span(c, HALF)
        early_copy(5, early_sum.at[here], early_sum.at[here], partner)

    def early_6():
        early_wait(5, early_sum.at[pl.ds(0, HALF)])

    early_0()
    gup[...] = jnp.zeros_like(gup)
    gdown_t[...] = jnp.zeros_like(gdown_t)
    gagain[...] = jnp.zeros_like(gagain)
    gtaps[...] = jnp.zeros_like(gtaps)

    def atm_back(i):
        here = pl.ds(pl.multiple_of(i * 128, 128), 128)
        cot = acot[pl.ds(i * 2, 2)].reshape(128, 256).astype(F32)
        out_grad = (cot + dot(gather[here, :], couple_t[...])).astype(BF16)
        gdown_t[...] += t_dot(out_grad, act[here, :])
        v = pre[here, :]
        s = sigmoid(v)
        pg = (dot(out_grad, down_t[...]) * (s * (1.0 + v * (1.0 - s)))).astype(BF16)
        gup[...] += t_dot(normed[here, :], pg)
        ng = dot(pg, up_t[...])
        u = unit[here, :]
        gagain[...] += jnp.sum(ng * u, axis=0, keepdims=True)
        gg = ng * again[...]
        sgrad[here, :] = inv_rms[here, 0:1] * (gg - u * jnp.mean(gg * u, axis=-1, keepdims=True))

    loop(2, atm_back)
    early_1()
    loop(2, lambda i: atm_back(i + 2))
    early_2()

    def taps_row(y):
        sg = sgrad[pl.ds(pl.multiple_of(y * breadth, breadth), breadth), :]
        for a in range(3):
            for b in range(3):
                gtaps[3 * a + b : 3 * a + b + 1, :] += jnp.sum(
                    sg * win[y + a, 7 + b : 7 + b + breadth, :], axis=0, keepdims=True
                )

    loop(height, taps_row)

    small[...] = jnp.zeros_like(small)
    small[0:9, :] = gtaps[0:9, 0:128]
    small[9:18, :] = gtaps[0:9, 128:256]
    small[18:19, :] = gagain[:, 0:128]
    small[19:20, :] = gagain[:, 128:256]
    small[20:21, :] = gogain[...]

    def small_phase(i, value, buf, at, peers):
        buf[at] = value
        for to in peers:
            remote(buf.at[at], buf.at[at], small_ssem.at[i], small_rsem.at[i], to).start()

    def small_wait(i, buf):
        rest = buf.shape[0] - 1
        both_ends(buf.at[pl.ds(0, rest)], small_ssem.at[i], small_rsem.at[i]).wait_recv()
        total = buf[0]
        for n in range(rest):
            total = total + buf[n + 1]
        return total

    small_phase(0, small[...], small_core, c, [partner])
    for i in range(4):
        late[256 * i : 256 * (i + 1), :] = gup[:, 128 * i : 128 * (i + 1)].astype(BF16)
        late[1024 + 256 * i : 1024 + 256 * (i + 1), :] = gdown_t[:, 128 * i : 128 * (i + 1)].astype(BF16)

    def send_late(i):
        to = offset_device(me, i + 1, 1)
        remote(late.at[span(rank_of(*to), PIECE)], pieces.at[i + 1], late_ssem, late_rsem, to).start()

    loop(DEVICES - 1, send_late)
    small_phase(1, small_wait(0, small_core), small_x, x, x_peers)
    early_3()
    mine = span(rank_of(tx, ty), PIECE)
    pieces[0] = late[mine, :]
    both_ends(pieces.at[pl.ds(1, DEVICES - 1)], late_ssem, late_rsem).wait_recv()

    def add(i, total):
        return total + jnp.sum(pieces[pl.ds(i * 8, 8)].astype(F32), axis=0)

    late_sum[mine, :] = lax.fori_loop(0, DEVICES // 8, add, jnp.zeros((PIECE, 128), F32)).astype(BF16)

    def send_sum(i):
        remote(late_sum.at[mine], late_sum.at[mine], sum_ssem, sum_rsem, offset_device(me, i + 1, 1)).start()

    small_phase(2, small_wait(1, small_x), small_y, y, y_peers)
    early_4()
    loop(DEVICES - 1, send_sum)
    small_phase(3, small_wait(2, small_y), small_z, z, z_peers)
    early_5()
    early_6()
    small[...] = small_wait(3, small_z)
    results = [
        pltpu.make_async_copy(early_sum, early_hbm, misc_sem.at[0]),
        pltpu.make_async_copy(small, small_hbm, misc_sem.at[2]),
        pltpu.make_async_copy(late_sum, late_hbm, misc_sem.at[3]),
    ]
    results[0].start()
    results[1].start()
    others = pl.ds(0, LATE - PIECE)
    both_ends(late_sum.at[others], sum_ssem, sum_rsem).wait_recv()
    results[2].start()
    both_ends(late.at[others], late_ssem, late_rsem).wait_send()
    both_ends(late.at[others], sum_ssem, sum_rsem).wait_send()
    for i, rows in ((0, 1), (1, 6), (2, 24), (3, 96)):
        both_ends(owners.at[pl.ds(0, rows)], own_ssem.at[i], own_rsem.at[i]).wait_send()
    for i, rows in enumerate((HALF, 3 * QUARTER, 3 * QUARTER, 3 * QUARTER, 3 * QUARTER, HALF)):
        sent = early_x if 0 < i < 4 else early
        both_ends(sent.at[pl.ds(0, rows)], early_ssem.at[i], early_rsem.at[i]).wait_send()
    for i, n in enumerate((1, 3, 3, 3)):
        both_ends(small_z.at[pl.ds(0, n)], small_ssem.at[i], small_rsem.at[i]).wait_send()

    sent = flux_out.at[pl.ds(ROWS, (DEVICES - 1) * ROWS)]
    pltpu.make_async_remote_copy(
        sent, sent, flux_ssem, flux_rsem.at[0], device_id=offset_device(me, 1, 1), device_id_type=MESH
    ).wait_send()
    sent = back_out.at[pl.ds(ROWS, (DEVICES - 1) * ROWS)]
    pltpu.make_async_remote_copy(
        sent, sent, back_ssem, back_rsem.at[0], device_id=offset_device(me, 1, 1), device_id_type=MESH
    ).wait_send()
    store.wait()
    for result in results:
        result.wait()


def finish(
    inv, anew_in, onew_arr, late, early, small, anew, onew, gtaps, gagain, gup, gdown, gcouple, gogain, goup, godown
):
    part = onew.shape[0]
    first = pl.program_id(0) * part

    def place(i):
        for j in range(8):
            onew[i * 8 + j] = onew_arr[inv[0, first + i * 8 + j] & 255]

    loop(part // 8, place)

    @pl.when(pl.program_id(0) == 0)
    def _():
        anew[...] = anew_in[...]
        for i in range(2):
            here = slice(128 * i, 128 * (i + 1))
            goup[:, here] = early[128 * i : 128 * (i + 1), :].astype(F32)
            godown[here, :] = early[256 + 128 * i : 256 + 128 * (i + 1), :].astype(F32).T
            gcouple[here, :] = early[512 + 128 * i : 512 + 128 * (i + 1), :].astype(F32).T
        for a in range(3):
            for i in range(2):
                gtaps[a, :, 128 * i : 128 * (i + 1)] = small[9 * i + 3 * a : 9 * i + 3 * a + 3, :]
        gagain[:, 0:128] = small[18:19, :]
        gagain[:, 128:256] = small[19:20, :]
        gogain[...] = small[20:21, :]
        for i in range(4):
            here = slice(128 * i, 128 * (i + 1))
            gup[:, here] = late[256 * i : 256 * (i + 1), :].astype(F32)
            gdown[here, :] = late[1024 + 256 * i : 1024 + 256 * (i + 1), :].astype(F32).T


def body(
    atm_state, kernel_taps, atm_gain, atm_up, atm_down, couple_weight, ocean_gain, ocean_up, ocean_down,
    ocean_state, land_mask, margin_cell, margin_area, owner_slot, atm_cotangent, ocean_cotangent,
):
    height, breadth, channels = atm_state.shape
    blocks = ocean_state.shape[0]
    n_rows = blocks * 32
    n_cells = height * breadth
    vmem, any_ = pl.BlockSpec(memory_space=pltpu.VMEM), pl.BlockSpec(memory_space=pl.ANY)
    block = lambda: pltpu.VMEM((blocks, 32, 128), BF16)
    flat = lambda: pltpu.VMEM((n_rows, 128), BF16)
    scratch = [
        block(), block(), block(),
        pltpu.VMEM((4, blocks // 4, 128), I32),
        pltpu.VMEM((4, blocks // 4, 128), F32),
        pltpu.VMEM((n_cells, n_rows), BF16),
        flat(), flat(), flat(), flat(),
        block(),
        pltpu.VMEM((DEVICES, blocks), I32),
        pltpu.VMEM((DEVICES, 128), I32),
        pltpu.SMEM((DEVICES, 128), I32),
        pltpu.VMEM((height + 2, breadth + 16, channels), F32),
        pltpu.VMEM((n_cells, 256), F32),
        pltpu.VMEM((n_cells, 128), F32),
        pltpu.VMEM((n_cells, 256), BF16),
        pltpu.VMEM((n_cells, 512), F32),
        pltpu.VMEM((n_cells, 512), BF16),
        pltpu.VMEM((n_cells, 128), BF16),
        pltpu.VMEM((128, n_cells), BF16),
        pltpu.VMEM((n_cells, 256), F32),
        pltpu.VMEM((512, 256), BF16),
        pltpu.VMEM((256, 512), BF16),
        pltpu.VMEM((128, 256), BF16),
        pltpu.VMEM((256, 128), BF16),
        pltpu.VMEM((128, 256), BF16),
        pltpu.VMEM((16, 256), F32),
        pltpu.VMEM((1, 256), F32),
        pltpu.VMEM((256, 512), F32),
        pltpu.VMEM((256, 512), F32),
        pltpu.VMEM((1, 128), F32),
        pltpu.VMEM((128, 256), F32),
        pltpu.VMEM((128, 256), F32),
        pltpu.VMEM((32, 128), F32),
        pltpu.VMEM((LATE, 128), BF16),
        pltpu.VMEM((DEVICES, PIECE, 128), BF16),
        pltpu.VMEM((LATE, 128), BF16),
        pltpu.VMEM((EARLY, 128), BF16),
        pltpu.VMEM((HALF, 128), BF16),
        pltpu.VMEM((HALF, 128), F32),
        pltpu.VMEM((HALF, 128), F32),
        pltpu.VMEM((HALF, 128), F32),
        pltpu.VMEM((HALF, 128), F32),
        pltpu.VMEM((EARLY, 128), BF16),
        pltpu.VMEM((2, 32, 128), F32),
        pltpu.VMEM((4, 32, 128), F32),
        pltpu.VMEM((4, 32, 128), F32),
        pltpu.VMEM((4, 32, 128), F32),
        pltpu.VMEM((16, channels), BF16),
        pltpu.VMEM((16, channels), BF16),
        pltpu.VMEM((breadth, channels), BF16),
        pltpu.VMEM((breadth, channels), BF16),
        pltpu.VMEM((6, 16, channels), BF16),
        pltpu.SemaphoreType.DMA((2,)),
        pltpu.SemaphoreType.DMA((8,)),
        pltpu.SemaphoreType.DMA((8,)),
        pltpu.SemaphoreType.DMA((4,)),
        pltpu.SemaphoreType.DMA((4,)),
        pltpu.SemaphoreType.DMA,
        pltpu.SemaphoreType.DMA((GROUPS,)),
        pltpu.SemaphoreType.DMA,
        pltpu.SemaphoreType.DMA((GROUPS,)),
        pltpu.SemaphoreType.DMA((4,)),
        pltpu.SemaphoreType.DMA,
        pltpu.SemaphoreType.DMA,
        pltpu.SemaphoreType.DMA,
        pltpu.SemaphoreType.DMA,
        pltpu.SemaphoreType.DMA((6,)),
        pltpu.SemaphoreType.DMA((6,)),
        pltpu.SemaphoreType.DMA((4,)),
        pltpu.SemaphoreType.DMA((4,)),
    ]
    anew, onew_arr, inv, late, early, small = pl.pallas_call(
        kernel,
        out_shape=[
            jax.ShapeDtypeStruct((height, breadth, channels), BF16),
            jax.ShapeDtypeStruct((blocks, 32, 128), BF16),
            jax.ShapeDtypeStruct((8, 256), I32),
            jax.ShapeDtypeStruct((LATE, 128), BF16),
            jax.ShapeDtypeStruct((EARLY, 128), BF16),
            jax.ShapeDtypeStruct((32, 128), F32),
        ],
        in_specs=[vmem] * 14 + [any_] * 2,
        out_specs=[vmem, any_, vmem, any_, any_, any_],
        scratch_shapes=scratch,
        compiler_params=pltpu.CompilerParams(
            collective_id=0, has_side_effects=True, vmem_limit_bytes=56 * 1024 * 1024
        ),
    )(
        atm_state, kernel_taps, atm_gain.reshape(1, -1), atm_up, atm_down, couple_weight,
        ocean_gain.reshape(1, -1), ocean_up, ocean_down, land_mask.T, margin_cell.transpose(1, 2, 0),
        margin_area.transpose(1, 2, 0), owner_slot.reshape(1, -1), atm_cotangent, ocean_state, ocean_cotangent,
    )
    part = blocks // 4
    whole = lambda *shape: pl.BlockSpec(shape, lambda i: (0,) * len(shape))
    anew, onew, gtaps, gagain, gup, gdown, gcouple, gogain, goup, godown = pl.pallas_call(
        finish,
        grid=(4,),
        out_shape=[
            jax.ShapeDtypeStruct((height, breadth, channels), BF16),
            jax.ShapeDtypeStruct((blocks, 32, 128), BF16),
            jax.ShapeDtypeStruct((3, 3, 256), F32),
            jax.ShapeDtypeStruct((1, 256), F32),
            jax.ShapeDtypeStruct((256, 512), F32),
            jax.ShapeDtypeStruct((512, 256), F32),
            jax.ShapeDtypeStruct((256, 128), F32),
            jax.ShapeDtypeStruct((1, 128), F32),
            jax.ShapeDtypeStruct((128, 256), F32),
            jax.ShapeDtypeStruct((256, 128), F32),
        ],
        in_specs=[
            pl.BlockSpec(memory_space=pltpu.SMEM),
            whole(height, breadth, channels), whole(blocks, 32, 128),
            whole(LATE, 128), whole(EARLY, 128), whole(32, 128),
        ],
        out_specs=[
            whole(height, breadth, channels), pl.BlockSpec((part, 32, 128), lambda i: (i, 0, 0)), whole(3, 3, 256),
            whole(1, 256), whole(256, 512), whole(512, 256), whole(256, 128), whole(1, 128), whole(128, 256),
            whole(256, 128),
        ],
        compiler_params=pltpu.CompilerParams(vmem_limit_bytes=60 * 1024 * 1024),
    )(inv, anew, onew_arr, late, early, small)
    return (
        anew, onew, gtaps, gagain.reshape(-1), gup, gdown, gcouple, gogain.reshape(-1), goup, godown,
    )


def solution(mesh):
    both = ("tx", "ty")
    return jax.shard_map(
        body,
        mesh=mesh,
        in_specs=(P("ty", "tx", None),) + (P(),) * 8 + (
            P(both, None, None), P(both, None), P(both, None, None), P(both, None, None), P(both),
            P("ty", "tx", None), P(both, None, None),
        ),
        out_specs=(P("ty", "tx", None), P(both, None, None)) + (P(),) * 8,
        check_vma=False,
    )
```

time: 140 us -> 120 us (0.86)
  Pallas kernels: 134 us -> 119 us
  local copies, waits for them, and re-layouts: 4.34 us -> 0 us
    pallas_call x1, Pallas kernels: 131 us -> 114 us  [body(): pl.pallas_call(kernel, out_shape=[jax.ShapeDtypeStruct((height, breadth,...]
    unnamed x8 -> x0, local copies, waits for them, and re-layouts: 4.34 us -> none
where the time goes in v3:
time: 120 us
  Pallas kernels  119 us (99%)
    pallas_call x1, Pallas kernels, body(): pl.pallas_call(kernel, out_shape=[jax.ShapeDtypeStruct((height, breadth,...  114 us
    pallas_call x1, Pallas kernels, body(): pl.pallas_call(finish, grid=(4,), out_shape=[jax.ShapeDtypeStruct((height...  4.93 us

profile of v3, /device:TPU:1, one launch (start us, length us, event | category | flops | bytes accessed | tf_op | source)
XLA Modules:
  0.0 119.7 jit_solution(9995821825705535920)
XLA Ops:
  0.6 114.1 %shard_map.231 = (bf16[8,64,256]{2,1,0:T(8,128)(2,1)}, bf16[256,32,128]{2,1,0:T(8,128)(2,1)}, s32[8,256]{1,0:T(8,128)}, bf16[2048,128]{1,0:T(8,128)(2,1)}, bf16[768,128]{1,0:T(8,128)(2,1)}, /*index=5*/f32[32,128]{1,0:T(8,128)}) custom-call(bf16[8,64,256]{2,1,0:T(8,128)(2,1)} %atm.1, f32[3,3,256]{2,1,0:T(4,128)} %taps.1, f32[1,256]{1,0:T(1,128)} %bitcast.11, ...), custom_call_target="tpu_custom_call" | custom-call | tf_op jit(solution)/shard_map/pallas_call | solution.py:706
  114.8 4.9 %shard_map.232 = (bf16[8,64,256]{2,1,0:T(8,128)(2,1)}, bf16[256,32,128]{2,1,0:T(8,128)(2,1)}, f32[3,3,256]{2,1,0:T(4,128)}, f32[1,256]{1,0:T(1,128)}, f32[256,51...) custom-call(s32[8,256]{1,0:T(8,128)} %get-tuple-element.26.inv, ...), custom_call_target="tpu_custom_call" | custom-call | tf_op jit(solution)/shard_map/pallas_call | solution.py:729

commit v4 on v3

--- a/solution.py
+++ b/solution.py
@@ -11,8 +11,6 @@
 MESH = pl.DeviceIdType.MESH
 F32, BF16, I32 = jnp.float32, jnp.bfloat16, jnp.int32
 DEVICES = 128
-MIX = 37
-UNMIX = pow(MIX, -1, DEVICES)
 ROWS = 64
 GROUP = 8
 GROUPS = DEVICES // GROUP
@@ -38,16 +36,35 @@
     return (div(x, 2) * 4 + z, rem(x, 2) * 8 + y * 2 + c)
 
 
-def offset_device(me, step, sign):
-    code = rem(step * MIX, DEVICES)
-    x = rem(me[0] + 4 + sign * rem(div(code, 2), 4), 4)
-    y = rem(me[1] + 4 + sign * rem(div(code, 8), 4), 4)
-    z = rem(me[2] + 4 + sign * div(code, 32), 4)
-    return device(x, y, z, rem(me[3] + code, 2))
+def group_devices(me, sign, low, turn, cores):
+    found = []
+    for j in range(GROUP):
+        dx, two = j % 4, j // 4 * 2
+        x = rem(me[0] + 4 + sign * dx, 4)
+        y = rem(me[1] + 8 + sign * (turn + dx), 4)
+        z = rem(me[2] + 8 + sign * (low + two + dx), 4)
+        found.append(device(x, y, z, cores))
+    return found
+
+
+def step_devices(me, g, sign):
+    return group_devices(me, sign, rem(div(g, 2), 2), div(g, 4), rem(me[3] + g, 2))
+
+
+def step_codes(g):
+    low, turn, dc = rem(div(g, 2), 2), div(g, 4), rem(g, 2)
+    return [
+        ((rem(low + j // 4 * 2 + j % 4, 4) * 4 + rem(turn + j % 4, 4)) * 4 + j % 4) * 2 + dc for j in range(GROUP)
+    ]
+
+
+def step_of(dx, dy, dz, dc):
+    t, turn = (dz - dx) & 3, (dy - dx) & 3
+    return (dc + 2 * (t & 1) + 4 * turn) * GROUP + dx + 4 * (t >> 1)
 
 
 def rank_of(tx, ty):
-    return rem((tx * 16 + ty) * MIX, DEVICES)
+    return rem(ty, 2) * (DEVICES // 2) + tx * 8 + div(ty, 2)
 
 
 def sigmoid(v):
@@ -72,14 +89,14 @@
 
 def kernel(
     atm, taps, again, up, down, couple, ogain, oup, odown, mask, margin_cell, margin_area, owner, acot, ostate_hbm, ocot_hbm,
-    anew, onew_hbm, inv_v, late_hbm, early_hbm, small_hbm,
-    ostate, ocot, wet, cells, shares, spread, flux_out, flux_in, back_out, back_in, onew_arr, owners, slots_v, slots_s,
-    win, unit, inv_rms, normed, pre, act, gather, coupled_t, sgrad, up_t, down_t, couple_t, oup_t, odown_t,
-    gtaps, gagain, gup, gdown_t, gogain, goup, godown_t, small, late, pieces, late_sum,
+    anew, onew_hbm, late_hbm, early_hbm, small_hbm,
+    ostate, ocot, wet, cells, shares, spread, flux_out, flux_in, back_out, back_in, onew, onew_arr, owners, slots_v, slots_s, inv_v, inv_s,
+    win, unit, inv_rms, normed, pre, act, gather, coupled_t, out_grad, pre_grad, act_t, normed_t, anew_t, sgrad, up_t, down_t, couple_t, oup_t, odown_t,
+    gtaps, gagain, gogain, goup, godown_t, small, late, pieces, late_sum,
     early, early_core, early_mine, early_x, early_y, early_z, early_sum, small_core, small_x, small_y, small_z,
     edge_w, edge_e, halo_n, halo_s, halo_c,
     load_sem, halo_ssem, halo_rsem, own_ssem, own_rsem, flux_ssem, flux_rsem, back_ssem, back_rsem, misc_sem,
-    late_ssem, late_rsem, sum_ssem, sum_rsem, early_ssem, early_rsem, small_ssem, small_rsem,
+    met, late_ssem, late_rsem, sum_ssem, sum_rsem, early_ssem, early_rsem, small_ssem, small_rsem,
 ):
     tx, ty = lax.axis_index("tx"), lax.axis_index("ty")
     me = digits(tx, ty)
@@ -98,14 +115,20 @@
     ys = [rem(me[1] + i, 4) for i in range(4)]
     zs = [rem(me[2] + i, 4) for i in range(4)]
     cs = [me[3], 1 - me[3]]
-    for i in range(1, DEVICES):
-        pl.semaphore_signal(
-            barrier, inc=1, device_id=device(xs[i // 2 % 4], ys[i // 8 % 4], zs[i // 32], cs[i % 2]), device_id_type=MESH
-        )
     partner = device(xs[0], ys[0], zs[0], cs[1])
     x_peers = [device(xs[i], ys[0], zs[0], cs[0]) for i in (1, 3, 2)]
     y_peers = [device(xs[0], ys[i], zs[0], cs[0]) for i in (1, 3, 2)]
     z_peers = [device(xs[0], ys[0], zs[i], cs[0]) for i in (1, 3, 2)]
+
+    te, tw, ts, tn = rem(tx + 1, 8), rem(tx + 7, 8), rem(ty + 1, 16), rem(ty + 15, 16)
+    around = [(tx, tn), (tx, ts)] + [(side, row) for side in (te, tw) for row in (tn, ty, ts)]
+    greeted = [partner] + x_peers + y_peers + z_peers + around
+    for to in greeted:
+        pl.semaphore_signal(barrier, inc=1, device_id=to, device_id_type=MESH)
+
+    def meet(i, peers):
+        for to in peers:
+            pl.semaphore_signal(met.at[i], inc=1, device_id=to, device_id_type=MESH)
 
     def remote(src, dst, ssem, rsem, to):
         return pltpu.make_async_remote_copy(src, dst, ssem, rsem, device_id=to, device_id_type=MESH)
@@ -126,9 +149,9 @@
     edge_w[...] = jnp.concatenate([west, nothing], axis=0).astype(BF16)
     edge_e[...] = jnp.concatenate([east, nothing], axis=0).astype(BF16)
 
-    pl.semaphore_wait(barrier, DEVICES - 1)
-
-    te, tw = (tx + 1) % 8, (tx + 7) % 8
+    pl.semaphore_wait(barrier, len(greeted))
+    meet(0, y_peers)
+
     north, south = ty > 0, ty < 15
 
     def halo(i, src, dst, dx, dy):
@@ -137,14 +160,14 @@
         )
 
     copies = [
-        (south, halo(0, atm.at[height - 1], halo_n, tx, (ty + 1) % 16)),
-        (north, halo(1, atm.at[0], halo_s, tx, (ty + 15) % 16)),
+        (south, halo(0, atm.at[height - 1], halo_n, tx, ts)),
+        (north, halo(1, atm.at[0], halo_s, tx, tn)),
         (None, halo(2, edge_e, halo_c.at[0], te, ty)),
         (None, halo(3, edge_w, halo_c.at[1], tw, ty)),
-        (south, halo(4, edge_e, halo_c.at[2], te, (ty + 1) % 16)),
-        (south, halo(5, edge_w, halo_c.at[3], tw, (ty + 1) % 16)),
-        (north, halo(6, edge_e, halo_c.at[4], te, (ty + 15) % 16)),
-        (north, halo(7, edge_w, halo_c.at[5], tw, (ty + 15) % 16)),
+        (south, halo(4, edge_e, halo_c.at[2], te, ts)),
+        (south, halo(5, edge_w, halo_c.at[3], tw, ts)),
+        (north, halo(6, edge_e, halo_c.at[4], te, tn)),
+        (north, halo(7, edge_w, halo_c.at[5], tw, tn)),
     ]
 
     def when(cond, f):
@@ -173,7 +196,7 @@
     t_tx, t_ty = slot >> 12, (slot >> 8) & 15
     theirs = ((t_tx >> 2) * 2 + (t_ty >> 3), (t_ty >> 1) & 3, t_tx & 3, t_ty & 1)
     dx, dy, dz, dc = [(t - m + n) & (n - 1) for t, m, n in zip(theirs, me, (4, 4, 4, 2))]
-    step = ((((dz * 4 + dy) * 4 + dx) * 2 + dc) * UNMIX) & (DEVICES - 1)
+    step = step_of(dx, dy, dz, dc)
     blocks = slot.shape[1]
     square = jnp.broadcast_to(step, (blocks, blocks))
     first = lax.broadcasted_iota(I32, square.shape, 0)
@@ -202,11 +225,28 @@
         shares[k] = got_share[k]
         cells[k] = got_cell[k].astype(I32)
 
-    for weight, turned in ((up, up_t), (down, down_t), (couple, couple_t), (oup, oup_t), (odown, odown_t)):
-        turned[...] = weight[...].astype(F32).T.astype(BF16)
-
+    pl.semaphore_wait(met.at[0], 3)
+    meet(1, z_peers)
     own_wait(0, 1, 1)
     own_phase(1, 2, x_peers)
+    def spread_columns(i):
+        here = pl.ds(pl.multiple_of(i * 128, 128), 128)
+        row = pl.ds(i, 1)
+        rows = lax.broadcasted_iota(I32, (n_cells // 16, 16, 128), 0) * 16 + lax.broadcasted_iota(
+            I32, (n_cells // 16, 16, 128), 1
+        )
+        rows = rows.astype(jnp.int16)
+        total = None
+        for k in range(4):
+            cell_k = jnp.broadcast_to(cells[k, row, :], (16, 128)).astype(jnp.int16)
+            share_k = jnp.broadcast_to(shares[k, row, :], (16, 128)).astype(BF16)
+            part = jnp.where(rows == cell_k[None], share_k[None], jnp.zeros((), BF16))
+            total = part if total is None else total + part
+        spread[:, here] = total.reshape(n_cells, 128)
+
+    couple_t[...] = couple[...].astype(F32).T.astype(BF16)
+    pl.semaphore_wait(met.at[1], 3)
+    meet(2, [partner])
 
     for cond, copy in copies:
         when(cond, copy.wait_send)
@@ -252,8 +292,6 @@
         normed[here, :] = (u * again[...]).astype(BF16)
 
     loop(height, stencil_row)
-    own_wait(1, 2, 3)
-    own_phase(2, 8, y_peers)
 
     def atm_mlp(i):
         here = pl.ds(pl.multiple_of(i * 128, 128), 128)
@@ -266,35 +304,27 @@
 
     loop(4, atm_mlp)
     coupled_t[...] = dot_t(couple_t[...], anew[...].reshape(n_cells, 256)).astype(BF16)
-    own_wait(2, 8, 3)
-    own_phase(3, 32, z_peers)
-
-    def spread_columns(i):
-        here = pl.ds(pl.multiple_of(i * 128, 128), 128)
-        rows = lax.broadcasted_iota(I32, (n_cells, 128), 0)
-        row = pl.ds(i, 1)
-        total = jnp.where(rows == cells[0, row, :], shares[0, row, :], 0.0)
-        for k in range(1, 4):
-            total = total + jnp.where(rows == cells[k, row, :], shares[k, row, :], 0.0)
-        spread[:, here] = total.astype(BF16)
-
-    def flux_copy(step, sign):
-        here = pl.ds(pl.multiple_of(step * ROWS, ROWS), ROWS)
-        return pltpu.make_async_remote_copy(
-            flux_out.at[here], flux_in.at[here], flux_ssem, flux_rsem.at[step // GROUP],
-            device_id=offset_device(me, step, sign), device_id_type=MESH,
-        )
+    own_wait(1, 2, 3)
+    own_phase(2, 8, y_peers)
+    pl.semaphore_wait(met.at[2], 1)
+
+    def send_group(g, sign, src, dst, ssem, rsem):
+        for j, to in enumerate(step_devices(me, g, sign)):
+            here = pl.ds(pl.multiple_of((g * GROUP + j) * ROWS, ROWS), ROWS)
+            copy = remote(src.at[here], dst.at[here], ssem, rsem.at[g], to)
+            when(g > 0 if j == 0 else None, copy.start)
 
     def flux_group(g):
         for j in range(GROUP // 2):
             spread_columns(g * (GROUP // 2) + j)
         here = pl.ds(pl.multiple_of(g * (GROUP * ROWS), GROUP * ROWS), GROUP * ROWS)
         flux_out[here, :] = dot(coupled_t[...], spread[:, here]).astype(BF16).T
-        pl.when(g > 0)(lambda: flux_copy(g * GROUP, 1).start())
-        for j in range(1, GROUP):
-            flux_copy(g * GROUP + j, 1).start()
-
-    loop(GROUPS, flux_group)
+        send_group(g, 1, flux_out, flux_in, flux_ssem, flux_rsem)
+
+    loop(GROUPS // 2, flux_group)
+    own_wait(2, 8, 3)
+    own_phase(3, 32, z_peers)
+    loop(GROUPS // 2, lambda g: flux_group(g + GROUPS // 2))
     flux_in[0:ROWS, :] = flux_out[0:ROWS, :]
 
     ones = jnp.ones((32, 128), BF16)
@@ -311,6 +341,11 @@
         wet[pl.ds(pl.multiple_of(i * 16, 16), 16)] = dot(wide, ones).astype(BF16).reshape(16, 32, 128)
 
     loop(16, wet_rows)
+
+    loop(16, wet_rows)
+
+    for weight, turned in ((oup, oup_t), (odown, odown_t)):
+        turned[...] = weight[...].astype(F32).T.astype(BF16)
 
     own_wait(3, 32, 3)
     owned = owners[...]
@@ -322,15 +357,21 @@
     two = jnp.max(jnp.where(hit, lane_f, -1.0), axis=1, keepdims=True)
     one = jnp.sum(jnp.where(lane_f == one, local, 0.0), axis=1, keepdims=True).astype(I32)
     two = jnp.sum(jnp.where(lane_f == two, local, 0.0), axis=1, keepdims=True).astype(I32)
-    position = 2 * ((lax.broadcasted_iota(I32, owned.shape, 0) * UNMIX) & (DEVICES - 1))
+    code = lax.broadcasted_iota(I32, owned.shape, 0)
+    position = 2 * step_of((code >> 1) & 3, (code >> 3) & 3, code >> 5, code & 1)
     found = jnp.where(one == lane, position, 0) + jnp.where(two == lane, position + 1, 0)
     inv_v[...] = jnp.broadcast_to(
         jnp.max(found.astype(F32), axis=0, keepdims=True).astype(I32), inv_v.shape
     )
     slots_v[...] = jnp.where(lane[:, 0:128] == 0, one, two)
-    to_scalar = pltpu.make_async_copy(slots_v, slots_s, misc_sem.at[0])
-    to_scalar.start()
-    to_scalar.wait()
+    to_scalar = [
+        pltpu.make_async_copy(slots_v, slots_s, misc_sem.at[0]),
+        pltpu.make_async_copy(inv_v, inv_s, misc_sem.at[4]),
+    ]
+    for copy in to_scalar:
+        copy.start()
+    for copy in to_scalar:
+        copy.wait()
     for load in loads:
         load.wait()
 
@@ -338,25 +379,13 @@
     godown_t[...] = jnp.zeros_like(godown_t)
     gogain[...] = jnp.zeros_like(gogain)
 
-    def back_copy(step, sign):
-        here = pl.ds(pl.multiple_of(step * ROWS, ROWS), ROWS)
-        return pltpu.make_async_remote_copy(
-            back_out.at[here], back_in.at[here], back_ssem, back_rsem.at[step // GROUP],
-            device_id=offset_device(me, step, sign), device_id_type=MESH,
-        )
-
     def wait_group(g, buf, ssem, rsem):
         def first():
-            some = buf.at[pl.ds(ROWS, (GROUP - 1) * ROWS)]
-            pltpu.make_async_remote_copy(
-                some, some, ssem, rsem.at[0], device_id=offset_device(me, 1, 1), device_id_type=MESH
-            ).wait_recv()
+            both_ends(buf.at[pl.ds(ROWS, (GROUP - 1) * ROWS)], ssem, rsem.at[0]).wait_recv()
 
         def later():
-            some = buf.at[pl.ds(pl.multiple_of(g * (GROUP * ROWS), GROUP * ROWS), GROUP * ROWS)]
-            pltpu.make_async_remote_copy(
-                some, some, ssem, rsem.at[g], device_id=offset_device(me, 1, 1), device_id_type=MESH
-            ).wait_recv()
+            here = pl.ds(pl.multiple_of(g * (GROUP * ROWS), GROUP * ROWS), GROUP * ROWS)
+            both_ends(buf.at[here], ssem, rsem.at[g]).wait_recv()
 
         pl.when(g == 0)(first)
         pl.when(g > 0)(later)
@@ -364,11 +393,11 @@
     def ocean_group(g):
         wait_group(g, flux_in, flux_ssem, flux_rsem)
         here = pl.ds(pl.multiple_of(g * (GROUP * ROWS), GROUP * ROWS), GROUP * ROWS)
-        codes = [rem((g * GROUP + j) * MIX, DEVICES) for j in range(GROUP)]
+        codes = step_codes(g)
         slot = [slots_s[codes[j // 2], j % 2] & 255 for j in range(2 * GROUP)]
         state = jnp.concatenate([ostate[s] for s in slot], axis=0).astype(F32)
         wets = jnp.concatenate([wet[s] for s in slot], axis=0)
-        out_grad = jnp.concatenate([ocot[s] for s in slot], axis=0) * wets
+        wet_cot = jnp.concatenate([ocot[s] for s in slot], axis=0) * wets
         total = state + flux_in[here, :].astype(F32)
         inv = lax.rsqrt(jnp.mean(total * total, axis=-1, keepdims=True) + EPS)
         u = total * inv
@@ -379,8 +408,8 @@
         onew_arr[pl.ds(g * (2 * GROUP), 2 * GROUP)] = (
             (state + wets.astype(F32) * dot(a, odown[...])).astype(BF16).reshape(2 * GROUP, 32, 128)
         )
-        godown_t[...] += t_dot(out_grad, a)
-        pg = (dot(out_grad, odown_t[...]) * (s * (1.0 + v * (1.0 - s)))).astype(BF16)
+        godown_t[...] += t_dot(wet_cot, a)
+        pg = (dot(wet_cot, odown_t[...]) * (s * (1.0 + v * (1.0 - s)))).astype(BF16)
         goup[...] += t_dot(nrm, pg)
         ng = dot(pg, oup_t[...])
         gogain[...] += jnp.sum(ng * u, axis=0, keepdims=True)
@@ -388,18 +417,22 @@
         tg = inv * (gg - u * jnp.mean(gg * u, axis=-1, keepdims=True))
         back_out[here, :] = tg.astype(BF16)
 
-        pl.when(g > 0)(lambda: back_copy(g * GROUP, -1).start())
-        for j in range(1, GROUP):
-            back_copy(g * GROUP + j, -1).start()
+        send_group(g, -1, back_out, back_in, back_ssem, back_rsem)
 
     loop(GROUPS, ocean_group)
     back_in[0:ROWS, :] = back_out[0:ROWS, :]
 
-    store = pltpu.make_async_copy(onew_arr, onew_hbm, misc_sem.at[1])
-    store.start()
     for i in range(2):
         early[128 * i : 128 * (i + 1), :] = goup[:, 128 * i : 128 * (i + 1)].astype(BF16)
-        early[256 + 128 * i : 256 + 128 * (i + 1), :] = godown_t[:, 128 * i : 128 * (i + 1)].astype(BF16)
+        early[256 + 128 * i : 256 + 128 * (i + 1), :] = godown_t[:, 128 * i : 128 * (i + 1)].T.astype(BF16)
+
+    for weight, turned in ((up, up_t), (down, down_t)):
+        turned[...] = weight[...].astype(F32).T.astype(BF16)
+    for i in range(4):
+        here = slice(128 * i, 128 * (i + 1))
+        act_t[:, here] = act[here, :].T
+        normed_t[:, here] = normed[here, :].T
+        anew_t[:, here] = anew[2 * i : 2 * i + 2].reshape(128, 256).T
 
     sgrad[:, 0:128] = jnp.zeros((n_cells, 128), F32)
 
@@ -411,9 +444,7 @@
     loop(GROUPS, back_group)
     gathered = sgrad[:, 0:128].astype(BF16)
     gather[...] = gathered
-    gcouple_t = t_dot(gathered, anew[...].reshape(n_cells, 256)).astype(BF16)
-    for i in range(2):
-        early[512 + 128 * i : 512 + 128 * (i + 1), :] = gcouple_t[:, 128 * i : 128 * (i + 1)]
+    early[512:768, :] = dot(anew_t[...], gathered).astype(BF16)
 
     x, y, z, c = me
 
@@ -471,30 +502,51 @@
         early_wait(5, early_sum.at[pl.ds(0, HALF)])
 
     early_0()
-    gup[...] = jnp.zeros_like(gup)
-    gdown_t[...] = jnp.zeros_like(gdown_t)
+    def send_late(low):
+        def group(g):
+            for j, to in enumerate(group_devices(me, 1, rem(g, 2), div(g, 2), low)):
+                copy = remote(
+                    late.at[span(rank_of(*to), PIECE)], pieces.at[(g * GROUP + j) * 2 + c], late_ssem, late_rsem, to
+                )
+                when(jnp.logical_or(g > 0, c != low) if j == 0 else None, copy.start)
+
+        loop(GROUPS // 2, group)
+
+    def atm_out_grad(i):
+        here = pl.ds(pl.multiple_of(i * 128, 128), 128)
+        cot = acot[pl.ds(i * 2, 2)].reshape(128, 256).astype(F32)
+        out_grad[here, :] = (cot + dot(gather[here, :], couple_t[...])).astype(BF16)
+
+    loop(4, atm_out_grad)
+    for i in range(2):
+        half = dot(act_t[...], out_grad[:, 128 * i : 128 * (i + 1)])
+        late[1024 + 512 * i : 1024 + 512 * (i + 1), :] = half.astype(BF16)
+    send_late(1)
+
+    def atm_back(i):
+        here = pl.ds(pl.multiple_of(i * 128, 128), 128)
+        v = pre[here, :]
+        s = sigmoid(v)
+        pre_grad[here, :] = (dot(out_grad[here, :], down_t[...]) * (s * (1.0 + v * (1.0 - s)))).astype(BF16)
+
+    loop(4, atm_back)
+    for i in range(4):
+        late[256 * i : 256 * (i + 1), :] = dot(normed_t[...], pre_grad[:, 128 * i : 128 * (i + 1)]).astype(BF16)
+    send_late(0)
+
     gagain[...] = jnp.zeros_like(gagain)
     gtaps[...] = jnp.zeros_like(gtaps)
 
-    def atm_back(i):
+    def atm_norm_back(i):
         here = pl.ds(pl.multiple_of(i * 128, 128), 128)
-        cot = acot[pl.ds(i * 2, 2)].reshape(128, 256).astype(F32)
-        out_grad = (cot + dot(gather[here, :], couple_t[...])).astype(BF16)
-        gdown_t[...] += t_dot(out_grad, act[here, :])
-        v = pre[here, :]
-        s = sigmoid(v)
-        pg = (dot(out_grad, down_t[...]) * (s * (1.0 + v * (1.0 - s)))).astype(BF16)
-        gup[...] += t_dot(normed[here, :], pg)
-        ng = dot(pg, up_t[...])
+        ng = dot(pre_grad[here, :], up_t[...])
         u = unit[here, :]
         gagain[...] += jnp.sum(ng * u, axis=0, keepdims=True)
         gg = ng * again[...]
         sgrad[here, :] = inv_rms[here, 0:1] * (gg - u * jnp.mean(gg * u, axis=-1, keepdims=True))
 
-    loop(2, atm_back)
+    loop(4, atm_norm_back)
     early_1()
-    loop(2, lambda i: atm_back(i + 2))
-    early_2()
 
     def taps_row(y):
         sg = sgrad[pl.ds(pl.multiple_of(y * breadth, breadth), breadth), :]
@@ -527,19 +579,19 @@
         return total
 
     small_phase(0, small[...], small_core, c, [partner])
-    for i in range(4):
-        late[256 * i : 256 * (i + 1), :] = gup[:, 128 * i : 128 * (i + 1)].astype(BF16)
-        late[1024 + 256 * i : 1024 + 256 * (i + 1), :] = gdown_t[:, 128 * i : 128 * (i + 1)].astype(BF16)
-
-    def send_late(i):
-        to = offset_device(me, i + 1, 1)
-        remote(late.at[span(rank_of(*to), PIECE)], pieces.at[i + 1], late_ssem, late_rsem, to).start()
-
-    loop(DEVICES - 1, send_late)
     small_phase(1, small_wait(0, small_core), small_x, x, x_peers)
+    early_2()
+
+    def place_blocks(i):
+        for j in range(8):
+            onew[i * 8 + j] = onew_arr[inv_s[0, i * 8 + j] & 255]
+
+    loop(blocks // 8, place_blocks)
+    store = pltpu.make_async_copy(onew, onew_hbm, misc_sem.at[1])
+    store.start()
     early_3()
     mine = span(rank_of(tx, ty), PIECE)
-    pieces[0] = late[mine, :]
+    pieces[c] = late[mine, :]
     both_ends(pieces.at[pl.ds(1, DEVICES - 1)], late_ssem, late_rsem).wait_recv()
 
     def add(i, total):
@@ -547,12 +599,14 @@
 
     late_sum[mine, :] = lax.fori_loop(0, DEVICES // 8, add, jnp.zeros((PIECE, 128), F32)).astype(BF16)
 
-    def send_sum(i):
-        remote(late_sum.at[mine], late_sum.at[mine], sum_ssem, sum_rsem, offset_device(me, i + 1, 1)).start()
+    def send_sum(g):
+        for j, to in enumerate(step_devices(me, g, 1)):
+            copy = remote(late_sum.at[mine], late_sum.at[mine], sum_ssem, sum_rsem, to)
+            when(g > 0 if j == 0 else None, copy.start)
 
     small_phase(2, small_wait(1, small_x), small_y, y, y_peers)
     early_4()
-    loop(DEVICES - 1, send_sum)
+    loop(GROUPS, send_sum)
     small_phase(3, small_wait(2, small_y), small_z, z, z_peers)
     early_5()
     early_6()
@@ -577,49 +631,62 @@
     for i, n in enumerate((1, 3, 3, 3)):
         both_ends(small_z.at[pl.ds(0, n)], small_ssem.at[i], small_rsem.at[i]).wait_send()
 
-    sent = flux_out.at[pl.ds(ROWS, (DEVICES - 1) * ROWS)]
-    pltpu.make_async_remote_copy(
-        sent, sent, flux_ssem, flux_rsem.at[0], device_id=offset_device(me, 1, 1), device_id_type=MESH
-    ).wait_send()
-    sent = back_out.at[pl.ds(ROWS, (DEVICES - 1) * ROWS)]
-    pltpu.make_async_remote_copy(
-        sent, sent, back_ssem, back_rsem.at[0], device_id=offset_device(me, 1, 1), device_id_type=MESH
-    ).wait_send()
+    both_ends(flux_out.at[pl.ds(ROWS, (DEVICES - 1) * ROWS)], flux_ssem, flux_rsem.at[0]).wait_send()
+    both_ends(back_out.at[pl.ds(ROWS, (DEVICES - 1) * ROWS)], back_ssem, back_rsem.at[0]).wait_send()
     store.wait()
     for result in results:
         result.wait()
 
 
-def finish(
-    inv, anew_in, onew_arr, late, early, small, anew, onew, gtaps, gagain, gup, gdown, gcouple, gogain, goup, godown
-):
-    part = onew.shape[0]
-    first = pl.program_id(0) * part
-
-    def place(i):
-        for j in range(8):
-            onew[i * 8 + j] = onew_arr[inv[0, first + i * 8 + j] & 255]
-
-    loop(part // 8, place)
-
-    @pl.when(pl.program_id(0) == 0)
-    def _():
-        anew[...] = anew_in[...]
+def finish(anew_in, onew_in, late_in, early_in, small_in, *refs):
+    outs, (anew, onew, late, early, small), (gtaps, gagain, gup, gdown, gcouple, gogain, goup, godown), sem, osem = (
+        refs[:10], refs[10:15], refs[15:23], refs[23], refs[24]
+    )
+    o_anew, o_onew, *o_grads = outs
+    n = onew.shape[0] // 4
+    parts = [pl.ds(i * n, n) for i in range(4)]
+    loads = [
+        pltpu.make_async_copy(src, dst, sem.at[i])
+        for i, (src, dst) in enumerate(
+            [(late_in, late), (early_in, early), (small_in, small), (anew_in, anew)]
+            + [(onew_in.at[p], onew.at[p]) for p in parts]
+        )
+    ]
+    for load in loads:
+        load.start()
+    stores = []
+
+    def put(src, dst):
+        stores.append(pltpu.make_async_copy(src, dst, osem.at[len(stores)]))
+        stores[-1].start()
+
+    loads[0].wait()
+    for i in range(4):
+        gup[:, 128 * i : 128 * (i + 1)] = late[256 * i : 256 * (i + 1), :].astype(F32)
+    put(gup, o_grads[2])
+    for i in range(2):
+        gdown[:, 128 * i : 128 * (i + 1)] = late[1024 + 512 * i : 1024 + 512 * (i + 1), :].astype(F32)
+    put(gdown, o_grads[3])
+    for load in loads[1:4]:
+        load.wait()
+    put(anew, o_anew)
+    for i in range(2):
+        goup[:, 128 * i : 128 * (i + 1)] = early[128 * i : 128 * (i + 1), :].astype(F32)
+    godown[...] = early[256:512, :].astype(F32)
+    gcouple[...] = early[512:768, :].astype(F32)
+    for a in range(3):
         for i in range(2):
-            here = slice(128 * i, 128 * (i + 1))
-            goup[:, here] = early[128 * i : 128 * (i + 1), :].astype(F32)
-            godown[here, :] = early[256 + 128 * i : 256 + 128 * (i + 1), :].astype(F32).T
-            gcouple[here, :] = early[512 + 128 * i : 512 + 128 * (i + 1), :].astype(F32).T
-        for a in range(3):
-            for i in range(2):
-                gtaps[a, :, 128 * i : 128 * (i + 1)] = small[9 * i + 3 * a : 9 * i + 3 * a + 3, :]
-        gagain[:, 0:128] = small[18:19, :]
-        gagain[:, 128:256] = small[19:20, :]
-        gogain[...] = small[20:21, :]
-        for i in range(4):
-            here = slice(128 * i, 128 * (i + 1))
-            gup[:, here] = late[256 * i : 256 * (i + 1), :].astype(F32)
-            gdown[here, :] = late[1024 + 256 * i : 1024 + 256 * (i + 1), :].astype(F32).T
+            gtaps[a, :, 128 * i : 128 * (i + 1)] = small[9 * i + 3 * a : 9 * i + 3 * a + 3, :]
+    gagain[:, 0:128] = small[18:19, :]
+    gagain[:, 128:256] = small[19:20, :]
+    gogain[...] = small[20:21, :]
+    for i in (0, 1, 4, 5, 6, 7):
+        put((gtaps, gagain, gup, gdown, gcouple, gogain, goup, godown)[i], o_grads[i])
+    for load, p in zip(loads[4:], parts):
+        load.wait()
+        put(onew.at[p], o_onew.at[p])
+    for store in stores:
+        store.wait()
 
 
 def body(
@@ -639,10 +706,12 @@
         pltpu.VMEM((4, blocks // 4, 128), F32),
         pltpu.VMEM((n_cells, n_rows), BF16),
         flat(), flat(), flat(), flat(),
-        block(),
+        block(), block(),
         pltpu.VMEM((DEVICES, blocks), I32),
         pltpu.VMEM((DEVICES, 128), I32),
         pltpu.SMEM((DEVICES, 128), I32),
+        pltpu.VMEM((8, blocks), I32),
+        pltpu.SMEM((8, blocks), I32),
         pltpu.VMEM((height + 2, breadth + 16, channels), F32),
         pltpu.VMEM((n_cells, 256), F32),
         pltpu.VMEM((n_cells, 128), F32),
@@ -651,6 +720,11 @@
         pltpu.VMEM((n_cells, 512), BF16),
         pltpu.VMEM((n_cells, 128), BF16),
         pltpu.VMEM((128, n_cells), BF16),
+        pltpu.VMEM((n_cells, 256), BF16),
+        pltpu.VMEM((n_cells, 512), BF16),
+        pltpu.VMEM((512, n_cells), BF16),
+        pltpu.VMEM((256, n_cells), BF16),
+        pltpu.VMEM((256, n_cells), BF16),
         pltpu.VMEM((n_cells, 256), F32),
         pltpu.VMEM((512, 256), BF16),
         pltpu.VMEM((256, 512), BF16),
@@ -659,8 +733,6 @@
         pltpu.VMEM((128, 256), BF16),
         pltpu.VMEM((16, 256), F32),
         pltpu.VMEM((1, 256), F32),
-        pltpu.VMEM((256, 512), F32),
-        pltpu.VMEM((256, 512), F32),
         pltpu.VMEM((1, 128), F32),
         pltpu.VMEM((128, 256), F32),
         pltpu.VMEM((128, 256), F32),
@@ -693,7 +765,8 @@
         pltpu.SemaphoreType.DMA((GROUPS,)),
         pltpu.SemaphoreType.DMA,
         pltpu.SemaphoreType.DMA((GROUPS,)),
-        pltpu.SemaphoreType.DMA((4,)),
+        pltpu.SemaphoreType.DMA((5,)),
+        pltpu.SemaphoreType.REGULAR((3,)),
         pltpu.SemaphoreType.DMA,
         pltpu.SemaphoreType.DMA,
         pltpu.SemaphoreType.DMA,
@@ -703,18 +776,17 @@
         pltpu.SemaphoreType.DMA((4,)),
         pltpu.SemaphoreType.DMA((4,)),
     ]
-    anew, onew_arr, inv, late, early, small = pl.pallas_call(
+    anew, onew, late, early, small = pl.pallas_call(
         kernel,
         out_shape=[
             jax.ShapeDtypeStruct((height, breadth, channels), BF16),
             jax.ShapeDtypeStruct((blocks, 32, 128), BF16),
-            jax.ShapeDtypeStruct((8, 256), I32),
             jax.ShapeDtypeStruct((LATE, 128), BF16),
             jax.ShapeDtypeStruct((EARLY, 128), BF16),
             jax.ShapeDtypeStruct((32, 128), F32),
         ],
         in_specs=[vmem] * 14 + [any_] * 2,
-        out_specs=[vmem, any_, vmem, any_, any_, any_],
+        out_specs=[vmem, any_, any_, any_, any_],
         scratch_shapes=scratch,
         compiler_params=pltpu.CompilerParams(
             collective_id=0, has_side_effects=True, vmem_limit_bytes=56 * 1024 * 1024
@@ -724,11 +796,8 @@
         ocean_gain.reshape(1, -1), ocean_up, ocean_down, land_mask.T, margin_cell.transpose(1, 2, 0),
         margin_area.transpose(1, 2, 0), owner_slot.reshape(1, -1), atm_cotangent, ocean_state, ocean_cotangent,
     )
-    part = blocks // 4
-    whole = lambda *shape: pl.BlockSpec(shape, lambda i: (0,) * len(shape))
     anew, onew, gtaps, gagain, gup, gdown, gcouple, gogain, goup, godown = pl.pallas_call(
         finish,
-        grid=(4,),
         out_shape=[
             jax.ShapeDtypeStruct((height, breadth, channels), BF16),
             jax.ShapeDtypeStruct((blocks, 32, 128), BF16),
@@ -741,18 +810,18 @@
             jax.ShapeDtypeStruct((128, 256), F32),
             jax.ShapeDtypeStruct((256, 128), F32),
         ],
-        in_specs=[
-            pl.BlockSpec(memory_space=pltpu.SMEM),
-            whole(height, breadth, channels), whole(blocks, 32, 128),
-            whole(LATE, 128), whole(EARLY, 128), whole(32, 128),
-        ],
-        out_specs=[
-            whole(height, breadth, channels), pl.BlockSpec((part, 32, 128), lambda i: (i, 0, 0)), whole(3, 3, 256),
-            whole(1, 256), whole(256, 512), whole(512, 256), whole(256, 128), whole(1, 128), whole(128, 256),
-            whole(256, 128),
+        in_specs=[any_] * 5,
+        out_specs=[any_] * 10,
+        scratch_shapes=[
+            pltpu.VMEM((height, breadth, channels), BF16), block(), pltpu.VMEM((LATE, 128), BF16),
+            pltpu.VMEM((EARLY, 128), BF16), pltpu.VMEM((32, 128), F32),
+            pltpu.VMEM((3, 3, 256), F32), pltpu.VMEM((1, 256), F32), pltpu.VMEM((256, 512), F32),
+            pltpu.VMEM((512, 256), F32), pltpu.VMEM((256, 128), F32), pltpu.VMEM((1, 128), F32),
+            pltpu.VMEM((128, 256), F32), pltpu.VMEM((256, 128), F32),
+            pltpu.SemaphoreType.DMA((8,)), pltpu.SemaphoreType.DMA((13,)),
         ],
         compiler_params=pltpu.CompilerParams(vmem_limit_bytes=60 * 1024 * 1024),
-    )(inv, anew, onew_arr, late, early, small)
+    )(anew, onew, late, early, small)
     return (
         anew, onew, gtaps, gagain.reshape(-1), gup, gdown, gcouple, gogain.reshape(-1), goup, godown,
     )

time: 120 us -> 116 us (0.967)
  Pallas kernels: 119 us -> 115 us
    pallas_call x1, Pallas kernels: 114 us -> 112 us  [body(): pl.pallas_call(kernel, out_shape=[jax.ShapeDtypeStruct((height, breadth,...]
    pallas_call x1, Pallas kernels: 4.93 us -> 3.17 us  [body(): pl.pallas_call(finish, out_shape=[jax.ShapeDtypeStruct((height, breadth,...]
where the time goes in v4:
time: 116 us
  Pallas kernels  115 us (99%)
    pallas_call x1, Pallas kernels, body(): pl.pallas_call(kernel, out_shape=[jax.ShapeDtypeStruct((height, breadth,...  112 us
    pallas_call x1, Pallas kernels, body(): pl.pallas_call(finish, out_shape=[jax.ShapeDtypeStruct((height, breadth,...  3.17 us

profile of v4, /device:TPU:1, one launch (start us, length us, event | category | flops | bytes accessed | tf_op | source)
XLA Modules:
  0.0 115.8 jit_solution(16232870689479218587)
XLA Ops:
  0.6 112.0 %shard_map.231 = (bf16[8,64,256]{2,1,0:T(8,128)(2,1)}, bf16[256,32,128]{2,1,0:T(8,128)(2,1)}, bf16[2048,128]{1,0:T(8,128)(2,1)}, bf16[768,128]{1,0:T(8,128)(2,1)}, f32[32,128]{1,0:T(8,128)}) custom-call(bf16[8,64,256]{2,1,0:T(8,128)(2,1)} %atm.1, f32[3,3,256]{2,1,0:T(4,128)} %taps.1, f32[1,256]{1,0:T(1,128)} %bitcast.11, bf16[256,512]{1,0:T(8,128)(2,1)} %up.1, ...), custom_call_target="tpu_custom_call" | custom-call | tf_op jit(solution)/shard_map/pallas_call | solution.py:779
  112.6 3.2 %shard_map.232 = (bf16[8,64,256]{2,1,0:T(8,128)(2,1)}, bf16[256,32,128]{2,1,0:T(8,128)(2,1)}, f32[3,3,256]{2,1,0:T(4,128)}, f32[1,256]{1,0:T(1,128)}, f32[256,51...) custom-call(bf16[8,64,256]{2,1,0:T(8,128)(2,1)} %get-tuple-element.2, ...), custom_call_target="tpu_custom_call" | custom-call | tf_op jit(solution)/shard_map/pallas_call | solution.py:799

commit v5 on v4

--- a/solution.py
+++ b/solution.py
@@ -14,6 +14,7 @@
 ROWS = 64
 GROUP = 8
 GROUPS = DEVICES // GROUP
+AHEAD = 9
 PIECE = 16
 LATE = DEVICES * PIECE
 EARLY = 768
@@ -321,29 +322,13 @@
         flux_out[here, :] = dot(coupled_t[...], spread[:, here]).astype(BF16).T
         send_group(g, 1, flux_out, flux_in, flux_ssem, flux_rsem)
 
-    loop(GROUPS // 2, flux_group)
+    loop(4, flux_group)
     own_wait(2, 8, 3)
     own_phase(3, 32, z_peers)
-    loop(GROUPS // 2, lambda g: flux_group(g + GROUPS // 2))
+    loop(AHEAD - 4, lambda g: flux_group(g + 4))
     flux_in[0:ROWS, :] = flux_out[0:ROWS, :]
 
-    ones = jnp.ones((32, 128), BF16)
-    wet_rows_of = mask[...].astype(F32).astype(BF16)
-
-    def wet_rows(i):
-        rows = lax.broadcasted_iota(I32, (512, blocks), 0)
-        cols = lax.broadcasted_iota(I32, (512, blocks), 1)
-        pick = (rows // 32 + i * 16 == cols).astype(F32).astype(BF16)
-        wide = dot_t(pick, wet_rows_of)
-        r2 = lax.broadcasted_iota(I32, wide.shape, 0)
-        c2 = lax.broadcasted_iota(I32, wide.shape, 1)
-        wide = jnp.where(r2 % 32 == c2, wide, 0.0).astype(BF16)
-        wet[pl.ds(pl.multiple_of(i * 16, 16), 16)] = dot(wide, ones).astype(BF16).reshape(16, 32, 128)
-
-    loop(16, wet_rows)
-
-    loop(16, wet_rows)
-
+    wet[...] = mask[...].astype(F32).T
     for weight, turned in ((oup, oup_t), (odown, odown_t)):
         turned[...] = weight[...].astype(F32).T.astype(BF16)
 
@@ -396,8 +381,10 @@
         codes = step_codes(g)
         slot = [slots_s[codes[j // 2], j % 2] & 255 for j in range(2 * GROUP)]
         state = jnp.concatenate([ostate[s] for s in slot], axis=0).astype(F32)
-        wets = jnp.concatenate([wet[s] for s in slot], axis=0)
-        wet_cot = jnp.concatenate([ocot[s] for s in slot], axis=0) * wets
+        eye = lax.broadcasted_iota(I32, (32, 32), 0) == lax.broadcasted_iota(I32, (32, 32), 1)
+        wets = jnp.concatenate([jnp.where(eye, wet[pl.ds(s, 1), :], 0.0) for s in slot], axis=0).astype(BF16)
+        wets = dot(wets, jnp.ones((32, 128), BF16))
+        wet_cot = jnp.concatenate([ocot[s] for s in slot], axis=0) * wets.astype(BF16)
         total = state + flux_in[here, :].astype(F32)
         inv = lax.rsqrt(jnp.mean(total * total, axis=-1, keepdims=True) + EPS)
         u = total * inv
@@ -406,7 +393,7 @@
         s = sigmoid(v)
         a = (v * s).astype(BF16)
         onew_arr[pl.ds(g * (2 * GROUP), 2 * GROUP)] = (
-            (state + wets.astype(F32) * dot(a, odown[...])).astype(BF16).reshape(2 * GROUP, 32, 128)
+            (state + wets * dot(a, odown[...])).astype(BF16).reshape(2 * GROUP, 32, 128)
         )
         godown_t[...] += t_dot(wet_cot, a)
         pg = (dot(wet_cot, odown_t[...]) * (s * (1.0 + v * (1.0 - s)))).astype(BF16)
@@ -419,7 +406,12 @@
 
         send_group(g, -1, back_out, back_in, back_ssem, back_rsem)
 
-    loop(GROUPS, ocean_group)
+    def both_groups(g):
+        flux_group(g + AHEAD)
+        ocean_group(g)
+
+    loop(GROUPS - AHEAD, both_groups)
+    loop(AHEAD, lambda g: ocean_group(g + GROUPS - AHEAD))
     back_in[0:ROWS, :] = back_out[0:ROWS, :]
 
     for i in range(2):
@@ -522,6 +514,7 @@
         half = dot(act_t[...], out_grad[:, 128 * i : 128 * (i + 1)])
         late[1024 + 512 * i : 1024 + 512 * (i + 1), :] = half.astype(BF16)
     send_late(1)
+    early_1()
 
     def atm_back(i):
         here = pl.ds(pl.multiple_of(i * 128, 128), 128)
@@ -546,7 +539,7 @@
         sgrad[here, :] = inv_rms[here, 0:1] * (gg - u * jnp.mean(gg * u, axis=-1, keepdims=True))
 
     loop(4, atm_norm_back)
-    early_1()
+    early_2()
 
     def taps_row(y):
         sg = sgrad[pl.ds(pl.multiple_of(y * breadth, breadth), breadth), :]
@@ -579,17 +572,9 @@
         return total
 
     small_phase(0, small[...], small_core, c, [partner])
+    early_3()
     small_phase(1, small_wait(0, small_core), small_x, x, x_peers)
-    early_2()
-
-    def place_blocks(i):
-        for j in range(8):
-            onew[i * 8 + j] = onew_arr[inv_s[0, i * 8 + j] & 255]
-
-    loop(blocks // 8, place_blocks)
-    store = pltpu.make_async_copy(onew, onew_hbm, misc_sem.at[1])
-    store.start()
-    early_3()
+
     mine = span(rank_of(tx, ty), PIECE)
     pieces[c] = late[mine, :]
     both_ends(pieces.at[pl.ds(1, DEVICES - 1)], late_ssem, late_rsem).wait_recv()
@@ -604,11 +589,20 @@
             copy = remote(late_sum.at[mine], late_sum.at[mine], sum_ssem, sum_rsem, to)
             when(g > 0 if j == 0 else None, copy.start)
 
+    loop(GROUPS // 2, send_sum)
+    early_4()
     small_phase(2, small_wait(1, small_x), small_y, y, y_peers)
-    early_4()
-    loop(GROUPS, send_sum)
+    loop(GROUPS // 2, lambda g: send_sum(g + GROUPS // 2))
+
+    def place_blocks(i):
+        for j in range(8):
+            onew[i * 8 + j] = onew_arr[inv_s[0, i * 8 + j] & 255]
+
+    loop(blocks // 8, place_blocks)
+    store = pltpu.make_async_copy(onew, onew_hbm, misc_sem.at[1])
+    store.start()
+    early_5()
     small_phase(3, small_wait(2, small_y), small_z, z, z_peers)
-    early_5()
     early_6()
     small[...] = small_wait(3, small_z)
     results = [
@@ -701,7 +695,8 @@
     block = lambda: pltpu.VMEM((blocks, 32, 128), BF16)
     flat = lambda: pltpu.VMEM((n_rows, 128), BF16)
     scratch = [
-        block(), block(), block(),
+        block(), block(),
+        pltpu.VMEM((blocks, 32), F32),
         pltpu.VMEM((4, blocks // 4, 128), I32),
         pltpu.VMEM((4, blocks // 4, 128), F32),
         pltpu.VMEM((n_cells, n_rows), BF16),

time: 116 us -> 111 us (0.957)
  Pallas kernels: 115 us -> 110 us
    pallas_call x1, Pallas kernels: 112 us -> 107 us  [body(): pl.pallas_call(kernel, out_shape=[jax.ShapeDtypeStruct((height, breadth,...]
where the time goes in v5:
time: 111 us
  Pallas kernels  110 us (99%)
    pallas_call x1, Pallas kernels, body(): pl.pallas_call(kernel, out_shape=[jax.ShapeDtypeStruct((height, breadth,...  107 us
    pallas_call x1, Pallas kernels, body(): pl.pallas_call(finish, out_shape=[jax.ShapeDtypeStruct((height, breadth,...  3.17 us

profile of v5, /device:TPU:1, one launch (start us, length us, event | category | flops | bytes accessed | tf_op | source)
XLA Modules:
  0.0 110.8 jit_solution(6977205066713824071)
XLA Ops:
  0.6 107.0 %shard_map.231 = (bf16[8,64,256]{2,1,0:T(8,128)(2,1)}, bf16[256,32,128]{2,1,0:T(8,128)(2,1)}, bf16[2048,128]{1,0:T(8,128)(2,1)}, bf16[768,128]{1,0:T(8,128)(2,1)}, f32[32,128]{1,0:T(8,128)}) custom-call(bf16[8,64,256]{2,1,0:T(8,128)(2,1)} %atm.1, f32[3,3,256]{2,1,0:T(4,128)} %taps.1, f32[1,256]{1,0:T(1,128)} %bitcast.11, bf16[256,512]{1,0:T(8,128)(2,1)} %up.1, ...), custom_call_target="tpu_custom_call" | custom-call | tf_op jit(solution)/shard_map/pallas_call | solution.py:774
  107.6 3.2 %shard_map.232 = (bf16[8,64,256]{2,1,0:T(8,128)(2,1)}, bf16[256,32,128]{2,1,0:T(8,128)(2,1)}, f32[3,3,256]{2,1,0:T(4,128)}, f32[1,256]{1,0:T(1,128)}, f32[256,51...) custom-call(bf16[8,64,256]{2,1,0:T(8,128)(2,1)} %get-tuple-element.2, ...), custom_call_target="tpu_custom_call" | custom-call | tf_op jit(solution)/shard_map/pallas_call | solution.py:794

commit v6 on v5

--- a/solution.py
+++ b/solution.py
@@ -572,8 +572,8 @@
         return total
 
     small_phase(0, small[...], small_core, c, [partner])
+    small_phase(1, small_wait(0, small_core), small_x, x, x_peers)
     early_3()
-    small_phase(1, small_wait(0, small_core), small_x, x, x_peers)
 
     mine = span(rank_of(tx, ty), PIECE)
     pieces[c] = late[mine, :]
@@ -589,10 +589,13 @@
             copy = remote(late_sum.at[mine], late_sum.at[mine], sum_ssem, sum_rsem, to)
             when(g > 0 if j == 0 else None, copy.start)
 
-    loop(GROUPS // 2, send_sum)
+    loop(4, send_sum)
+    small_phase(2, small_wait(1, small_x), small_y, y, y_peers)
     early_4()
-    small_phase(2, small_wait(1, small_x), small_y, y, y_peers)
-    loop(GROUPS // 2, lambda g: send_sum(g + GROUPS // 2))
+    loop(6, lambda g: send_sum(g + 4))
+    small_phase(3, small_wait(2, small_y), small_z, z, z_peers)
+    early_5()
+    loop(6, lambda g: send_sum(g + 10))
 
     def place_blocks(i):
         for j in range(8):
@@ -601,8 +604,6 @@
     loop(blocks // 8, place_blocks)
     store = pltpu.make_async_copy(onew, onew_hbm, misc_sem.at[1])
     store.start()
-    early_5()
-    small_phase(3, small_wait(2, small_y), small_z, z, z_peers)
     early_6()
     small[...] = small_wait(3, small_z)
     results = [

time: 111 us -> 113 us (1.018)
  Pallas kernels: 110 us -> 112 us
    pallas_call x1, Pallas kernels: 107 us -> 109 us  [body(): pl.pallas_call(kernel, out_shape=[jax.ShapeDtypeStruct((height, breadth,...]
where the time goes in v6:
time: 113 us
  Pallas kernels  112 us (99%)
    pallas_call x1, Pallas kernels, body(): pl.pallas_call(kernel, out_shape=[jax.ShapeDtypeStruct((height, breadth,...  109 us
    pallas_call x1, Pallas kernels, body(): pl.pallas_call(finish, out_shape=[jax.ShapeDtypeStruct((height, breadth,...  3.17 us

profile of v6, /device:TPU:1, one launch (start us, length us, event | category | flops | bytes accessed | tf_op | source)
XLA Modules:
  0.0 112.8 jit_solution(4041518378717433472)
XLA Ops:
  0.6 109.0 %shard_map.231 = (bf16[8,64,256]{2,1,0:T(8,128)(2,1)}, bf16[256,32,128]{2,1,0:T(8,128)(2,1)}, bf16[2048,128]{1,0:T(8,128)(2,1)}, bf16[768,128]{1,0:T(8,128)(2,1)}, f32[32,128]{1,0:T(8,128)}) custom-call(bf16[8,64,256]{2,1,0:T(8,128)(2,1)} %atm.1, f32[3,3,256]{2,1,0:T(4,128)} %taps.1, f32[1,256]{1,0:T(1,128)} %bitcast.11, bf16[256,512]{1,0:T(8,128)(2,1)} %up.1, ...), custom_call_target="tpu_custom_call" | custom-call | tf_op jit(solution)/shard_map/pallas_call | solution.py:775
  109.6 3.2 %shard_map.232 = (bf16[8,64,256]{2,1,0:T(8,128)(2,1)}, bf16[256,32,128]{2,1,0:T(8,128)(2,1)}, f32[3,3,256]{2,1,0:T(4,128)}, f32[1,256]{1,0:T(1,128)}, f32[256,51...) custom-call(bf16[8,64,256]{2,1,0:T(8,128)(2,1)} %get-tuple-element.2, ...), custom_call_target="tpu_custom_call" | custom-call | tf_op jit(solution)/shard_map/pallas_call | solution.py:795
